TPU v7x, 256 devices: a whole 4x4x8 slice. The times are simulated.
256 devices in a mesh: px: 16 (over y, x), py: 16 (over z, core).
Axes of the slice: x: 4, y: 4, z: 8, core: 2. Of those that a mesh axis runs over, the one named last changes fastest.
Arguments:
- point_features: bfloat16 [262144, 64], P(('px', 'py')), may hold values from -6 to 6
- positions: bfloat16 [262144, 3], P(('px', 'py')), may hold values from -1 to 1
- targets: bfloat16 [262144], P(('px', 'py')), may hold values from -6 to 6
- routes: int32 [262144, 1], P(('px', 'py')), may hold values from 0 to 255; in each aligned block of 1024 rows (0 to 1023, 1024 to 2047, ...) at most 8 rows name the same one
- live_counts: int32 [256], P(('px', 'py')), may hold values from 512 to 1024, as said below
- cell_neighbours: int32 [128, 64, 2048], P('px', 'py'), may hold values from 0 to 2047
- cell_counts: int32 [128, 64, 256], P('px', 'py'), may hold values from 1 to 8
- slot_neighbours: int32 [256, 8192], P(('px', 'py')), may hold values from 0 to 8191
- encoder_in: float32 [3, 80], replicated, may hold values from -4 to 4
- encoder_bias: float32 [80], replicated, may hold values from -4 to 4
- encoder_out: bfloat16 [80, 64], replicated, may hold values from -0.625 to 0.625
- decoder_in: float32 [3, 256], replicated, may hold values from -4 to 4
- decoder_bias: float32 [256], replicated, may hold values from -4 to 4
- decoder_out: bfloat16 [256, 64], replicated, may hold values from -0.375 to 0.375
- skip_weight: bfloat16 [64, 64], replicated, may hold values from -0.75 to 0.75
- spectral_weight: bfloat16 [32, 32, 16, 64, 128], P(None, 'px', 'py'), may hold values from -6 to 6
- readout_weight: float32 [64], replicated, may hold values from -3 to 3
Outputs:
- prediction: float32 [256, 2048], P(('px', 'py'))
- spectral_grad: float32 [32, 32, 16, 64, 128], P(None, 'px', 'py')
Inputs may be any that keep to these rules, and one draw needn't show every extreme that they name: `routes`: owner of a point, a mesh index px * 16 + py. Among the rows of one block no owner is named by more than 8 rows. `live_counts`: points of a block from this count on are padding and go nowhere. `cell_neighbours`: A slot index source block times 8 plus rank, of the owner of the cell; entries from cell_counts on are unused. `slot_neighbours`: A local cell index of the owner.
All inputs are finite; a program needn't handle non-finite values.
Results may differ from a plain program's by a relative error of at most 0.014.
Values may be sent and summed in bfloat16 or wider, within the bound.
A program may use at most 128 MiB of HBM per device.

v0:
```python
import math

import jax
import jax.numpy as jnp
from jax import lax
from jax.sharding import PartitionSpec as P

PRECISE = lax.Precision.HIGHEST
HALF_ROOT = 0.7071067811865476
GAUSS_NORM = 0.3989422804014327


def shortened(value):
    return jax.tree.map(lambda a: a.astype(jnp.bfloat16) if a.dtype == jnp.float32 else a, value)


def silu_of(values):
    return values / (1.0 + jnp.exp(-values))


def gelu_of(values):
    return 0.5 * values * (1.0 + lax.erf(values * HALF_ROOT))


def gelu_slope(values):
    return (
        0.5 * (1.0 + lax.erf(values * HALF_ROOT))
        + values * jnp.exp(-0.5 * values * values) * GAUSS_NORM
    )


def slot_ranks(target):
    ordering = jnp.argsort(target, stable=True)
    ordered = target[ordering]
    starts = jnp.searchsorted(ordered, ordered, side="left")
    within = jnp.arange(target.shape[0], dtype=jnp.int32) - starts
    return jnp.zeros(target.shape, jnp.int32).at[ordering].set(within)


def pack_sends(features, extras, target, counted, capacity, devices):
    living = jnp.arange(target.shape[0], dtype=jnp.int32) < counted
    target = jnp.where(living, target, devices)
    placement = target * capacity + slot_ranks(target)
    outgoing = (
        jnp.zeros((devices * capacity, features.shape[1]), features.dtype)
        .at[placement]
        .set(features, mode="drop")
    )
    side_data = (
        jnp.zeros((devices * capacity, extras.shape[1]), extras.dtype)
        .at[placement]
        .set(extras, mode="drop")
    )
    return (outgoing, side_data)


def cell_centres(rows_x, rows_y, depth_cells):
    position_ids = jnp.arange(rows_x * rows_y * depth_cells, dtype=jnp.int32)
    along_x = (position_ids // (rows_y * depth_cells)).astype(jnp.float32)
    along_y = (position_ids // depth_cells % rows_y).astype(jnp.float32)
    along_z = (position_ids % depth_cells).astype(jnp.float32)
    return jnp.stack(
        [
            (along_x + 0.5) * (2.0 / rows_x) - 1.0,
            (along_y + 0.5) * (2.0 / rows_y) - 1.0,
            (along_z + 0.5) * (2.0 / depth_cells) - 1.0,
        ],
        1,
    )


def kernel_hidden(offset, weight_in, bias):
    summed = (
        offset[:, 0:1] * weight_in[0]
        + offset[:, 1:2] * weight_in[1]
        + offset[:, 2:3] * weight_in[2]
        + bias
    )
    return silu_of(summed).astype(jnp.bfloat16)


def encode_cells(
    slot_features, slot_places, neighbours, counted, centres, weight_in, bias, weight_out
):
    per_cell = neighbours.shape[1]
    flat_ids = neighbours.reshape(-1)
    nearby = slot_features[flat_ids]
    offset = slot_places[flat_ids].astype(jnp.float32) - jnp.repeat(centres, per_cell, axis=0)
    hidden = kernel_hidden(offset, weight_in, bias)
    kernel = jnp.dot(hidden, weight_out, preferred_element_type=jnp.float32)
    summands = (kernel * nearby.astype(jnp.float32)).reshape(neighbours.shape[0], per_cell, -1)
    kept_mask = jnp.arange(per_cell, dtype=jnp.int32)[None, :] < counted[:, None]
    summed = jnp.sum(jnp.where(kept_mask[:, :, None], summands, 0.0), axis=1)
    return (summed / counted[:, None].astype(jnp.float32)).astype(jnp.bfloat16)


def decode_slots(
    activated, slot_side, neighbours, centres, weight_in, bias, weight_out, readout_weight
):
    per_slot = neighbours.shape[1]
    flat_ids = neighbours.reshape(-1)
    nearby = activated[flat_ids]
    places = slot_side[:, 0:3].astype(jnp.float32)
    offset = jnp.repeat(places, per_slot, axis=0) - centres[flat_ids]
    hidden = kernel_hidden(offset, weight_in, bias)
    kernel = jnp.dot(hidden, weight_out, preferred_element_type=jnp.float32)
    blended = (
        jnp.sum(
            (kernel * nearby.astype(jnp.float32)).reshape(neighbours.shape[0], per_slot, -1), axis=1
        )
        / per_slot
    )
    living = slot_side[:, 4].astype(jnp.float32)
    predicted = living * jnp.sum(blended * readout_weight, axis=1)
    residue = living * (predicted - slot_side[:, 3].astype(jnp.float32))
    shares = kernel * (jnp.repeat(residue, per_slot) / per_slot)[:, None] * readout_weight
    return (predicted, shares)


def apply_modes(x_real, x_imag, weights):
    channels = x_real.shape[3]
    w_real = weights[..., :channels].astype(jnp.float32)
    w_imag = weights[..., channels:].astype(jnp.float32)

    def mixing(left, right):
        return jnp.einsum("rpqc,rpqco->rpqo", left, right, precision=PRECISE)

    return (
        mixing(x_real, w_real) - mixing(x_imag, w_imag),
        mixing(x_real, w_imag) + mixing(x_imag, w_real),
    )


def twiddle(length, frequency):
    steps_along = jnp.arange(length, dtype=jnp.int32)
    turns = steps_along[:, None] * frequency[None, :] % length
    angles = turns.astype(jnp.float32) * (2.0 * math.pi / length)
    return (jnp.cos(angles), jnp.sin(angles))


def signed_frequency(modes):
    counted = jnp.arange(2 * modes, dtype=jnp.int32)
    return jnp.where(counted < modes, counted, counted - 2 * modes)


def contract(form, left, right):
    return jnp.einsum(form, left, right, precision=PRECISE)


def forward_modes(grid_field, modes, depth_modes):
    rows_x, rows_y, depth_cells, channels = grid_field.shape
    total_x = rows_x * lax.axis_size("px")
    total_y = rows_y * lax.axis_size("py")
    scaling = 1.0 / math.sqrt(total_x * total_y * depth_cells)
    depth_cos, depth_sin = twiddle(depth_cells, jnp.arange(depth_modes, dtype=jnp.int32))
    z_real = contract("ijlc,lq->ijqc", grid_field, depth_cos)
    z_imag = -contract("ijlc,lq->ijqc", grid_field, depth_sin)
    arrived = lax.all_to_all(
        jnp.concatenate([z_real, z_imag], 3), "py", split_axis=2, concat_axis=1, tiled=True
    )
    z_real = arrived[..., :channels]
    z_imag = arrived[..., channels:]
    frequency = signed_frequency(modes)
    col_cos, col_sin = twiddle(total_y, frequency)
    y_real = contract("ijqc,jp->ipqc", z_real, col_cos) + contract("ijqc,jp->ipqc", z_imag, col_sin)
    y_imag = contract("ijqc,jp->ipqc", z_imag, col_cos) - contract("ijqc,jp->ipqc", z_real, col_sin)
    arrived = lax.all_to_all(
        jnp.concatenate([y_real, y_imag], 3), "px", split_axis=1, concat_axis=0, tiled=True
    )
    y_real = arrived[..., :channels]
    y_imag = arrived[..., channels:]
    row_cos, row_sin = twiddle(total_x, frequency)
    x_real = contract("ipqc,ir->rpqc", y_real, row_cos) + contract("ipqc,ir->rpqc", y_imag, row_sin)
    x_imag = contract("ipqc,ir->rpqc", y_imag, row_cos) - contract("ipqc,ir->rpqc", y_real, row_sin)
    return (x_real * scaling, x_imag * scaling)


def inverse_modes(v_real, v_imag, rows_x, rows_y, depth_cells):
    channels = v_real.shape[3]
    modes = v_real.shape[0] // 2
    depth_modes = v_real.shape[2] * lax.axis_size("py")
    total_x = rows_x * lax.axis_size("px")
    total_y = rows_y * lax.axis_size("py")
    scaling = 1.0 / math.sqrt(total_x * total_y * depth_cells)
    frequency = signed_frequency(modes)
    row_cos, row_sin = twiddle(total_x, frequency)
    y_real = contract("rpqc,ir->ipqc", v_real, row_cos) - contract("rpqc,ir->ipqc", v_imag, row_sin)
    y_imag = contract("rpqc,ir->ipqc", v_real, row_sin) + contract("rpqc,ir->ipqc", v_imag, row_cos)
    arrived = lax.all_to_all(
        jnp.concatenate([y_real, y_imag], 3).astype(jnp.bfloat16),
        "px",
        split_axis=0,
        concat_axis=1,
        tiled=True,
    ).astype(jnp.float32)
    y_real = arrived[..., :channels]
    y_imag = arrived[..., channels:]
    col_cos, col_sin = twiddle(total_y, frequency)
    z_real = contract("ipqc,jp->ijqc", y_real, col_cos) - contract("ipqc,jp->ijqc", y_imag, col_sin)
    z_imag = contract("ipqc,jp->ijqc", y_real, col_sin) + contract("ipqc,jp->ijqc", y_imag, col_cos)
    arrived = lax.all_to_all(
        shortened(jnp.concatenate([z_real, z_imag], 3)),
        "py",
        split_axis=1,
        concat_axis=2,
        tiled=True,
    )
    z_real = arrived[..., :channels]
    z_imag = arrived[..., channels:]
    depth_ids = jnp.arange(depth_modes, dtype=jnp.int32)
    doubling = jnp.where(depth_ids == 0, 1.0, 2.0).astype(jnp.float32) * scaling
    depth_cos, depth_sin = twiddle(depth_cells, depth_ids)
    return contract("ijqc,lq->ijlc", z_real, depth_cos * doubling) - contract(
        "ijqc,lq->ijlc", z_imag, depth_sin * doubling
    )


def body(
    point_features,
    positions,
    targets,
    routes,
    live_counts,
    cell_neighbours,
    cell_counts,
    slot_neighbours,
    encoder_in,
    encoder_bias,
    encoder_out,
    decoder_in,
    decoder_bias,
    decoder_out,
    skip_weight,
    spectral_weight,
    readout_weight,
):
    span_x = lax.axis_size("px")
    span_y = lax.axis_size("py")
    devices = span_x * span_y
    points, channels = point_features.shape
    capacity = 2 * points // devices
    extras = jnp.concatenate([positions, targets[:, None], jnp.ones((points, 1), jnp.bfloat16)], 1)
    outgoing, side_data = pack_sends(
        point_features, extras, routes[:, 0], live_counts[0], capacity, devices
    )
    outgoing = outgoing.reshape(span_x, span_y * capacity, channels)
    side_data = side_data.reshape(span_x, span_y * capacity, 5)
    arrived, arrived_side = (
        lax.all_to_all(
            lax.all_to_all(outgoing, "px", split_axis=0, concat_axis=0, tiled=True),
            "py",
            split_axis=1,
            concat_axis=1,
            tiled=True,
        ),
        lax.all_to_all(
            lax.all_to_all(side_data, "px", split_axis=0, concat_axis=0, tiled=True),
            "py",
            split_axis=1,
            concat_axis=1,
            tiled=True,
        ),
    )
    slot_total = devices * capacity
    arrived = arrived.reshape(slot_total, channels)
    arrived_side = arrived_side.reshape(slot_total, 5)
    rows_x, rows_y, depth_lists = cell_neighbours.shape
    depth_cells = cell_counts.shape[2]
    per_cell = depth_lists // depth_cells
    cell_total = rows_x * rows_y * depth_cells
    centres = cell_centres(rows_x, rows_y, depth_cells)

    def encode_row(inputs_now):
        row_lists, row_counts, row_centres = inputs_now
        return encode_cells(
            arrived,
            arrived_side[:, 0:3],
            row_lists,
            row_counts,
            row_centres,
            encoder_in,
            encoder_bias,
            encoder_out,
        )

    latent = lax.map(
        encode_row,
        (
            cell_neighbours.reshape(rows_x, rows_y * depth_cells, per_cell),
            cell_counts.reshape(rows_x, rows_y * depth_cells),
            centres.reshape(rows_x, rows_y * depth_cells, 3),
        ),
    )
    latent = latent.reshape(rows_x, rows_y, depth_cells, channels)
    modes = spectral_weight.shape[0] // 2
    local_modes = spectral_weight.shape[2]
    depth_modes = local_modes * span_y
    x_real, x_imag = forward_modes(latent.astype(jnp.float32), modes, depth_modes)
    v_real, v_imag = apply_modes(x_real, x_imag, spectral_weight)
    spectral_part = inverse_modes(v_real, v_imag, rows_x, rows_y, depth_cells)
    skip_part = jnp.dot(
        latent.reshape(cell_total, channels), skip_weight, preferred_element_type=jnp.float32
    )
    before = spectral_part.reshape(cell_total, channels) + skip_part
    activated = gelu_of(before).astype(jnp.bfloat16)
    per_slot = slot_neighbours.shape[1] // slot_total
    blocks = slot_total // 1024

    def decode_step(running, inputs_now):
        block_side, block_lists = inputs_now
        predicted, shares = decode_slots(
            activated,
            block_side,
            block_lists,
            centres,
            decoder_in,
            decoder_bias,
            decoder_out,
            readout_weight,
        )
        running = running + jax.ops.segment_sum(
            shares, block_lists.reshape(-1), num_segments=cell_total
        )
        return (running, predicted)

    grid_grad, predicted = lax.scan(
        decode_step,
        jnp.zeros((cell_total, channels), jnp.float32),
        (arrived_side.reshape(blocks, 1024, 5), slot_neighbours.reshape(blocks, 1024, per_slot)),
    )
    before_grad = (grid_grad * gelu_slope(before)).reshape(rows_x, rows_y, depth_cells, channels)
    g_real, g_imag = forward_modes(before_grad, modes, depth_modes)
    depth_ids = lax.axis_index("py") * local_modes + jnp.arange(local_modes, dtype=jnp.int32)
    doubling = jnp.where(depth_ids == 0, 1.0, 2.0).astype(jnp.float32)[None, None, :, None]
    g_real = g_real * doubling
    g_imag = g_imag * doubling
    grad_real = (
        x_real[..., :, None] * g_real[..., None, :] + x_imag[..., :, None] * g_imag[..., None, :]
    )
    grad_imag = (
        x_real[..., :, None] * g_imag[..., None, :] - x_imag[..., :, None] * g_real[..., None, :]
    )
    return (predicted.reshape(1, slot_total), jnp.concatenate([grad_real, grad_imag], 4))


def solution(mesh):
    in_specs = (
        P(("px", "py"), None),
        P(("px", "py"), None),
        P(("px", "py")),
        P(("px", "py"), None),
        P(("px", "py")),
        P("px", "py", None),
        P("px", "py", None),
        P(("px", "py"), None),
        P(),
        P(),
        P(),
        P(),
        P(),
        P(),
        P(),
        P(None, "px", "py", None, None),
        P(),
    )
    out_specs = (P(("px", "py"), None), P(None, "px", "py", None, None))
    return jax.shard_map(body, mesh=mesh, in_specs=in_specs, out_specs=out_specs, check_vma=False)
```

profile of v0, /device:TPU:1, one launch (start us, length us, event | category | flops | bytes accessed | tf_op | source)
XLA Modules:
  0.0 1004.2 jit_solution(12230208656166348296)
XLA Ops:
  11.6 50.7 %while.49 = (s32[]{:T(128)}, u32[1024]{0:T(1024)S(1)}, u32[1024]{0:T(1024)S(1)}, s32[1024]{0:T(1024)S(1)}, s32[]{:T(128)}, /*index=5*/s32[]{:T(128)}, s32[]{}) while((s32[]{:T(128)}, u32[1024]{0:T(1024)S(1)}, u32[1024]{0:T(1024)S(1)}, s32[1024]{0:T(1024)S(1)}, s32[]{:T(128)}, /*index=5*/s32[]{:T(128)}, s32[]{}) %tuple.108), condition=%wide.region_2.3_spmd.clone, body=%wide.region_1.2_spmd.clone.sunk | while | flops 19460 | bytes 67685 | solution.py:35
  71.3 7.6 all-to-all-start
  97.5 11.1 %all-to-all-start.1 = ((bf16[16,2,320]{2,1,0:T(2,128)(2,1)}), bf16[16,2,320]{2,1,0:T(2,128)(2,1)S(1)}, u32[]{:S(2)}, u32[]{:S(2)}) async-start(bf16[16,2,320]{2,1,0:T(2,128)(2,1)} %reshape.932), calls=%async_computation.1 | async-start | bytes 49152 | tf_op jit(solution)/shard_map/all_to_all | solution.py:256
  132.3 581.5 %while.47 = (s32[]{:T(128)}, bf16[8,1024,64]{2,1,0:T(8,128)(2,1)}, s32[8,1024]{1,0:T(8,128)S(1)}, bf16[2048,5]{1,0:T(8,128)(2,1)S(1)}, s32[8,1024,8]{2,1,0:T(8,1...) while((s32[]{:T(128)}, bf16[8,1024,64]{2,1,0:T(8,128)(2,1)}, ...), condition=%wide.region_8.9_spmd, body=%wide.region_6.8_spmd.sunk | while | flops 92693504 | bytes 15705433 | solution.py:286
  135.1 24.0 %gather_fusion.1 = bf16[8192,3]{1,0:T(8,128)(2,1)S(1)} fusion(bf16[2048,3]{1,0:T(8,128)(2,1)S(1)} %bitcast.337, s32[8192]{0:T(1024)S(1)} %broadcast_clamp_fusion.7), kind=kCustom, calls=%fused_computation.1.clone.1 | custom fusion | bytes 131072 | tf_op jit(solution)/shard_map/while/body/eval_jaxpr/gather | solution.py:88
  166.0 24.0 %gather_fusion = bf16[8192,64]{1,0:T(8,128)(2,1)S(1)} fusion(bf16[2048,64]{1,0:T(8,128)(2,1)S(1)} %get-tuple-element.661, s32[8192]{0:T(1024)S(1)} %broadcast_clamp_fusion.7), kind=kCustom, calls=%fused_computation.2.clone.1 | custom fusion | bytes 2129920 | tf_op jit(solution)/shard_map/while/body/eval_jaxpr/gather | solution.py:87
  197.1 7.0 fusion.341
  207.7 24.0 %gather_fusion.1 = bf16[8192,3]{1,0:T(8,128)(2,1)S(1)} fusion(bf16[2048,3]{1,0:T(8,128)(2,1)S(1)} %bitcast.337, s32[8192]{0:T(1024)S(1)} %broadcast_clamp_fusion.7), kind=kCustom, calls=%fused_computation.1.clone.1 | custom fusion | bytes 131072 | tf_op jit(solution)/shard_map/while/body/eval_jaxpr/gather | solution.py:88
  238.6 24.0 %gather_fusion = bf16[8192,64]{1,0:T(8,128)(2,1)S(1)} fusion(bf16[2048,64]{1,0:T(8,128)(2,1)S(1)} %get-tuple-element.661, s32[8192]{0:T(1024)S(1)} %broadcast_clamp_fusion.7), kind=kCustom, calls=%fused_computation.2.clone.1 | custom fusion | bytes 2129920 | tf_op jit(solution)/shard_map/while/body/eval_jaxpr/gather | solution.py:87
  280.4 24.0 %gather_fusion.1 = bf16[8192,3]{1,0:T(8,128)(2,1)S(1)} fusion(bf16[2048,3]{1,0:T(8,128)(2,1)S(1)} %bitcast.337, s32[8192]{0:T(1024)S(1)} %broadcast_clamp_fusion.7), kind=kCustom, calls=%fused_computation.1.clone.1 | custom fusion | bytes 131072 | tf_op jit(solution)/shard_map/while/body/eval_jaxpr/gather | solution.py:88
  311.3 24.0 %gather_fusion = bf16[8192,64]{1,0:T(8,128)(2,1)S(1)} fusion(bf16[2048,64]{1,0:T(8,128)(2,1)S(1)} %get-tuple-element.661, s32[8192]{0:T(1024)S(1)} %broadcast_clamp_fusion.7), kind=kCustom, calls=%fused_computation.2.clone.1 | custom fusion | bytes 2129920 | tf_op jit(solution)/shard_map/while/body/eval_jaxpr/gather | solution.py:87
  353.0 24.0 %gather_fusion.1 = bf16[8192,3]{1,0:T(8,128)(2,1)S(1)} fusion(bf16[2048,3]{1,0:T(8,128)(2,1)S(1)} %bitcast.337, s32[8192]{0:T(1024)S(1)} %broadcast_clamp_fusion.7), kind=kCustom, calls=%fused_computation.1.clone.1 | custom fusion | bytes 131072 | tf_op jit(solution)/shard_map/while/body/eval_jaxpr/gather | solution.py:88
  383.9 24.0 %gather_fusion = bf16[8192,64]{1,0:T(8,128)(2,1)S(1)} fusion(bf16[2048,64]{1,0:T(8,128)(2,1)S(1)} %get-tuple-element.661, s32[8192]{0:T(1024)S(1)} %broadcast_clamp_fusion.7), kind=kCustom, calls=%fused_computation.2.clone.1 | custom fusion | bytes 2129920 | tf_op jit(solution)/shard_map/while/body/eval_jaxpr/gather | solution.py:87
  425.6 24.0 %gather_fusion.1 = bf16[8192,3]{1,0:T(8,128)(2,1)S(1)} fusion(bf16[2048,3]{1,0:T(8,128)(2,1)S(1)} %bitcast.337, s32[8192]{0:T(1024)S(1)} %broadcast_clamp_fusion.7), kind=kCustom, calls=%fused_computation.1.clone.1 | custom fusion | bytes 131072 | tf_op jit(solution)/shard_map/while/body/eval_jaxpr/gather | solution.py:88
  456.5 24.0 %gather_fusion = bf16[8192,64]{1,0:T(8,128)(2,1)S(1)} fusion(bf16[2048,64]{1,0:T(8,128)(2,1)S(1)} %get-tuple-element.661, s32[8192]{0:T(1024)S(1)} %broadcast_clamp_fusion.7), kind=kCustom, calls=%fused_computation.2.clone.1 | custom fusion | bytes 2129920 | tf_op jit(solution)/shard_map/while/body/eval_jaxpr/gather | solution.py:87
  498.2 24.0 %gather_fusion.1 = bf16[8192,3]{1,0:T(8,128)(2,1)S(1)} fusion(bf16[2048,3]{1,0:T(8,128)(2,1)S(1)} %bitcast.337, s32[8192]{0:T(1024)S(1)} %broadcast_clamp_fusion.7), kind=kCustom, calls=%fused_computation.1.clone.1 | custom fusion | bytes 131072 | tf_op jit(solution)/shard_map/while/body/eval_jaxpr/gather | solution.py:88
  529.2 24.0 %gather_fusion = bf16[8192,64]{1,0:T(8,128)(2,1)S(1)} fusion(bf16[2048,64]{1,0:T(8,128)(2,1)S(1)} %get-tuple-element.661, s32[8192]{0:T(1024)S(1)} %broadcast_clamp_fusion.7), kind=kCustom, calls=%fused_computation.2.clone.1 | custom fusion | bytes 2129920 | tf_op jit(solution)/shard_map/while/body/eval_jaxpr/gather | solution.py:87
  570.9 24.0 %gather_fusion.1 = bf16[8192,3]{1,0:T(8,128)(2,1)S(1)} fusion(bf16[2048,3]{1,0:T(8,128)(2,1)S(1)} %bitcast.337, s32[8192]{0:T(1024)S(1)} %broadcast_clamp_fusion.7), kind=kCustom, calls=%fused_computation.1.clone.1 | custom fusion | bytes 131072 | tf_op jit(solution)/shard_map/while/body/eval_jaxpr/gather | solution.py:88
  601.8 24.0 %gather_fusion = bf16[8192,64]{1,0:T(8,128)(2,1)S(1)} fusion(bf16[2048,64]{1,0:T(8,128)(2,1)S(1)} %get-tuple-element.661, s32[8192]{0:T(1024)S(1)} %broadcast_clamp_fusion.7), kind=kCustom, calls=%fused_computation.2.clone.1 | custom fusion | bytes 2129920 | tf_op jit(solution)/shard_map/while/body/eval_jaxpr/gather | solution.py:87
  643.5 24.0 %gather_fusion.1 = bf16[8192,3]{1,0:T(8,128)(2,1)S(1)} fusion(bf16[2048,3]{1,0:T(8,128)(2,1)S(1)} %bitcast.337, s32[8192]{0:T(1024)S(1)} %broadcast_clamp_fusion.7), kind=kCustom, calls=%fused_computation.1.clone.1 | custom fusion | bytes 131072 | tf_op jit(solution)/shard_map/while/body/eval_jaxpr/gather | solution.py:88
  674.4 24.0 %gather_fusion = bf16[8192,64]{1,0:T(8,128)(2,1)S(1)} fusion(bf16[2048,64]{1,0:T(8,128)(2,1)S(1)} %get-tuple-element.661, s32[8192]{0:T(1024)S(1)} %broadcast_clamp_fusion.7), kind=kCustom, calls=%fused_computation.2.clone.1 | custom fusion | bytes 2129920 | tf_op jit(solution)/shard_map/while/body/eval_jaxpr/gather | solution.py:87
  721.9 11.0 %all-to-all-done.4 = f32[8,4,16,128]{3,1,0,2:T(4,128)S(1)} async-done(((f32[8,4,16,128]{3,1,0,2:T(4,128)}), f32[8,4,16,128]{3,1,0,2:T(4,128)S(1)}, u32[]{:S(2)}, u32[]{:S(2)}) %all-to-all-start.4) | async-done | bytes 262176 | tf_op jit(solution)/shard_map/all_to_all | solution.py:158
  739.2 7.3 all-to-all-done.5
  797.1 155.1 %while.48 = (s32[]{:T(128)}, f32[8192,64]{1,0:T(8,128)}, f32[2,1024]{1,0:T(2,128)S(1)}, s32[2,1024,4]{2,1,0:T(8,128)}, bf16[2,1024,5]{1,2,0:T(8,128)(2,1)S(1)}, ...) while((s32[]{:T(128)}, f32[8192,64]{1,0:T(8,128)}, ...), condition=%wide.region_13.14_spmd, body=%wide.region_9.13_spmd.sunk | while | flops 146380864 | bytes 19246264 | solution.py:326
  800.2 12.1 %gather_fusion.2 = bf16[4096,64]{1,0:T(8,128)(2,1)S(1)} fusion(bf16[8192,64]{1,0:T(8,128)(2,1)S(1)} %get-tuple-element.700, s32[4096]{0:T(1024)S(1)} %broadcast_clamp_fusion.8), kind=kCustom, calls=%fused_computation.4.clone.1 | custom fusion | bytes 1064960 | tf_op jit(solution)/shard_map/while/body/eval_jaxpr/gather | solution.py:102
  816.2 16.3 %gather_fusion.3 = f32[4096,3]{1,0:T(8,128)} fusion(f32[8192,3]{1,0:T(8,128)} %get-tuple-element.696, s32[4096]{0:T(1024)S(1)} %broadcast_clamp_fusion.8), kind=kCustom, calls=%fused_computation.3.clone.1 | custom fusion | bytes 114688 | tf_op jit(solution)/shard_map/while/body/eval_jaxpr/gather | solution.py:104
  850.3 24.6 %scatter_fusion = f32[8192,64]{1,0:T(8,128)} fusion(f32[8192,64]{1,0:T(8,128)} %get-tuple-element.678, s32[4096]{0:T(1024)S(1)} %reshape.962, f32[4096,64]{1,0:T(8,128)} %copy.453), kind=kCustom, calls=%fused_computation.6.clone.1 | custom fusion | flops 262144 | bytes 3162112 | tf_op jit(solution)/shard_map/while/body/eval_jaxpr/scatter-add | solution.py:321
  877.6 12.1 %gather_fusion.2 = bf16[4096,64]{1,0:T(8,128)(2,1)S(1)} fusion(bf16[8192,64]{1,0:T(8,128)(2,1)S(1)} %get-tuple-element.700, s32[4096]{0:T(1024)S(1)} %broadcast_clamp_fusion.8), kind=kCustom, calls=%fused_computation.4.clone.1 | custom fusion | bytes 1064960 | tf_op jit(solution)/shard_map/while/body/eval_jaxpr/gather | solution.py:102
  893.7 16.3 %gather_fusion.3 = f32[4096,3]{1,0:T(8,128)} fusion(f32[8192,3]{1,0:T(8,128)} %get-tuple-element.696, s32[4096]{0:T(1024)S(1)} %broadcast_clamp_fusion.8), kind=kCustom, calls=%fused_computation.3.clone.1 | custom fusion | bytes 114688 | tf_op jit(solution)/shard_map/while/body/eval_jaxpr/gather | solution.py:104
  927.7 24.6 %scatter_fusion = f32[8192,64]{1,0:T(8,128)} fusion(f32[8192,64]{1,0:T(8,128)} %get-tuple-element.678, s32[4096]{0:T(1024)S(1)} %reshape.962, f32[4096,64]{1,0:T(8,128)} %copy.453), kind=kCustom, calls=%fused_computation.6.clone.1 | custom fusion | flops 262144 | bytes 3162112 | tf_op jit(solution)/shard_map/while/body/eval_jaxpr/scatter-add | solution.py:321
  969.5 15.9 %all_to_all.128 = f32[8,4,16,128]{3,1,0,2:T(4,128)S(1)} all-to-all(f32[8,4,16,128]{3,1,0,2:T(4,128)S(1)} %copy.350), channel_id=1, replica_groups=mesh['px'=16,'py'=16] {'py'}, dimensions={2} | all-to-all | bytes 524288 | tf_op jit(solution)/shard_map/all_to_all | solution.py:158
  992.2 7.1 all-to-all-done.9
  (475 shorter events, 441.8 us)
Async XLA Ops:
  0.6 789.3 %copy-start = (bf16[64,64]{1,0:T(8,128)(2,1)S(1)}, bf16[64,64]{1,0:T(8,128)(2,1)}, u32[]{:S(2)}) copy-start(bf16[64,64]{1,0:T(8,128)(2,1)} %param.37) | copy-start | bytes 24580
  11.6 50.9 %copy-start.23 = (bf16[1024,3]{0,1:T(4,128)(2,1)S(1)}, bf16[1024,3]{0,1:T(4,128)(2,1)}, u32[]{:S(2)}) copy-start(bf16[1024,3]{0,1:T(4,128)(2,1)} %param.24) | copy-start | bytes 18436
  11.6 55.5 %copy-start.21 = (s32[1024,1]{0,1:T(1,128)S(1)}, s32[1024,1]{0,1:T(1,128)}, u32[]{:S(2)}) copy-start(s32[1024,1]{0,1:T(1,128)} %param.26) | copy-start | bytes 12292
  11.6 67.2 %copy-start.10 = (bf16[1024,64]{0,1:T(8,128)(2,1)S(1)}, bf16[1024,64]{0,1:T(8,128)(2,1)}, u32[]{:S(2)}) copy-start(bf16[1024,64]{0,1:T(8,128)(2,1)} %param.23) | copy-start | bytes 393220
  71.3 14.1 %all-to-all-start = ((bf16[16,128,5]{1,2,0:T(8,128)(2,1)}), bf16[16,128,5]{1,2,0:T(8,128)(2,1)S(1)}, u32[]{:S(2)}, u32[]{:S(2)}) async-start(bf16[16,128,5]{1,2,0:T(8,128)(2,1)} %copy.316), calls=%async_computation | async-start | bytes 65536 | tf_op jit(solution)/shard_map/all_to_all | solution.py:257
  82.4 37.7 %copy-start.18 = (s32[8,4,256]{2,1,0:T(4,128)S(1)}, s32[8,4,256]{2,1,0:T(4,128)}, u32[]{:S(2)}) copy-start(s32[8,4,256]{2,1,0:T(4,128)} %param.29) | copy-start | bytes 98308
  82.4 37.7 %copy-start.9 = (s32[8,4,2048]{2,1,0:T(4,128)S(1)}, s32[8,4,2048]{2,1,0:T(4,128)}, u32[]{:S(2)}) copy-start(s32[8,4,2048]{2,1,0:T(4,128)} %param.28) | copy-start | bytes 786436
  85.3 12.2 %all-to-all-start.2 = ((bf16[16,128,64]{1,2,0:T(8,128)(2,1)}), bf16[16,128,64]{1,2,0:T(8,128)(2,1)S(1)}, u32[]{:S(2)}, u32[]{:S(2)}) async-start(bf16[16,128,64]{1,2,0:T(8,128)(2,1)} %copy.321), calls=%async_computation.2 | async-start | bytes 524288 | tf_op jit(solution)/shard_map/all_to_all | solution.py:250
  97.5 18.5 %all-to-all-start.1 = ((bf16[16,2,320]{2,1,0:T(2,128)(2,1)}), bf16[16,2,320]{2,1,0:T(2,128)(2,1)S(1)}, u32[]{:S(2)}, u32[]{:S(2)}) async-start(bf16[16,2,320]{2,1,0:T(2,128)(2,1)} %reshape.932), calls=%async_computation.1 | async-start | bytes 49152 | tf_op jit(solution)/shard_map/all_to_all | solution.py:256
  116.0 15.8 %all-to-all-start.3 = ((bf16[16,2,4096]{2,1,0:T(2,128)(2,1)}), bf16[16,2,4096]{2,1,0:T(2,128)(2,1)S(1)}, u32[]{:S(2)}, u32[]{:S(2)}) async-start(bf16[16,2,4096]{2,1,0:T(2,128)(2,1)} %reshape.934), calls=%async_computation.3 | async-start | bytes 524288 | tf_op jit(solution)/shard_map/all_to_all | solution.py:249
  123.7 8.6 copy-start.20
  123.7 8.6 copy-start.28
  124.1 8.1 copy-start.5
  197.1 7.9 copy-start.16
  269.7 7.9 copy-start.16
  342.4 7.9 copy-start.16
  415.0 7.9 copy-start.16
  487.6 7.9 copy-start.16
  560.3 7.9 copy-start.16
  632.9 7.9 copy-start.16
  705.5 7.9 copy-start.16
  718.5 14.5 %all-to-all-start.4 = ((f32[8,4,16,128]{3,1,0,2:T(4,128)}), f32[8,4,16,128]{3,1,0,2:T(4,128)S(1)}, u32[]{:S(2)}, u32[]{:S(2)}) async-start(f32[8,4,16,128]{3,1,0,2:T(4,128)} %copy.329), calls=%async_computation.4 | async-start | bytes 524288 | tf_op jit(solution)/shard_map/all_to_all | solution.py:158
  721.9 43.6 %copy-start.7 = (s32[32]{0:T(128)}, s32[32]{0:T(128)S(1)}, u32[]{:S(2)}) copy-start(s32[32]{0:T(128)S(1)} %compare_select_fusion.6) | copy-start | bytes 388
  733.0 14.2 %copy-start.24 = (bf16[32,2,1,64,128]{4,3,2,1,0:T(8,128)(2,1)S(1)}, bf16[32,2,1,64,128]{4,3,2,1,0:T(8,128)(2,1)}, u32[]{:S(2)}) copy-start(bf16[32,2,1,64,128]{4,3,2,1,0:T(8,128)(2,1)} %param.38) | copy-start | bytes 3145732
  735.6 11.0 %all-to-all-start.5 = ((f32[8,32,1,128]{3,0,2,1:T(8,128)}), f32[8,32,1,128]{3,0,2,1:T(8,128)S(1)}, u32[]{:S(2)}, u32[]{:S(2)}) async-start(f32[8,32,1,128]{3,0,2,1:T(8,128)} %copy.333), calls=%async_computation.5 | async-start | bytes 262144 | tf_op jit(solution)/shard_map/all_to_all | solution.py:167
  751.8 21.1 %copy-start.19 = (s32[1,8192]{1,0:T(1,128)S(1)}, s32[1,8192]{1,0:T(1,128)}, u32[]{:S(2)}) copy-start(s32[1,8192]{1,0:T(1,128)} %param.30) | copy-start | bytes 98308
  754.0 10.0 all-to-all-start.6
  766.8 14.6 %all-to-all-start.7 = ((bf16[8,64,1,128]{3,0,2,1:T(8,128)(2,1)}), bf16[8,64,1,128]{3,0,2,1:T(8,128)(2,1)S(1)}, u32[]{:S(2)}, u32[]{:S(2)}) async-start(bf16[8,64,1,128]{3,0,2,1:T(8,128)(2,1)} %copy.340), calls=%async_computation.7 | async-start | bytes 262144 | tf_op jit(solution)/shard_map/all_to_all | solution.py:201
  969.2 16.3 %copy-start.8 = (s32[32]{0:T(128)S(1)}, s32[32]{0:T(128)}, u32[]{:S(2)}) copy-start(s32[32]{0:T(128)} %copy-done.7) | copy-start | bytes 388
  985.4 6.2 copy-start.12
  985.4 6.2 copy-start.14
  988.0 11.3 %all-to-all-start.9 = ((f32[8,32,1,128]{3,0,2,1:T(8,128)}), f32[8,32,1,128]{3,0,2,1:T(8,128)S(1)}, u32[]{:S(2)}, u32[]{:S(2)}) async-start(f32[8,32,1,128]{3,0,2,1:T(8,128)} %copy.354), calls=%async_computation.9 | async-start | bytes 262144 | tf_op jit(solution)/shard_map/all_to_all | solution.py:167
  (28 other events, 52.4 us)
where the time goes:
time: 1010 us; the launch traced here: 1000 us
  local copies, waits for them, and re-layouts  671 us (66%)
  other arithmetic  152 us (15%)
  matrix products  58 us (6%)
  waiting for transfers between devices  55.5 us (5%)
  starting transfers between devices  46.8 us (5%)
  blocking collectives  15.9 us (2%)
    gather x16, local copies, waits for them, and re-layouts, encode_cells(): nearby = slot_features[flat_ids]  205 us
    gather x8, local copies, waits for them, and re-layouts, encode_cells(): slot_places[flat_ids].astype(jnp.float32)  192 us
    reduce_sum x8, other arithmetic, encode_cells(): summed = jnp.sum(jnp.where(kept_mask[:, :, None], summands, 0.0), axis=1)  55.6 us
    gather x11, local copies, waits for them, and re-layouts, slot_ranks(): starts = jnp.searchsorted(ordered, ordered, side='left')  49.8 us
    slice x10, local copies, waits for them, and re-layouts, kernel_hidden(): offset[:, 0:1] * weight_in[0] + offset[:, 1:2] * weight_in[1]  49.4 us
    scatter-add x2, other arithmetic, decode_step(): jax.ops.segment_sum(shares, block_lists.reshape(-1), num_segments=cell_to...  49.1 us
    gather x2, local copies, waits for them, and re-layouts, decode_slots(): offset = jnp.repeat(places, per_slot, axis=0) - centres[flat_ids]  32.6 us
    gather x4, local copies, waits for them, and re-layouts, decode_slots(): nearby = activated[flat_ids]  26.6 us
  transfers between devices with their start and end apart: 9, of which 9 were waited for; matrix products, arithmetic and copies ran while one was open for 2% of the time, Pallas kernels for 0%

commit v1 on v0

v1 whole, which is shorter than its diff:
```python
import functools
import math

import jax
import jax.numpy as jnp
import numpy as np
from jax import lax
from jax.experimental import pallas as pl
from jax.experimental.pallas import tpu as pltpu
from jax.sharding import PartitionSpec as P

MESH = pl.DeviceIdType.MESH
HALF_ROOT = 0.7071067811865476
GAUSS_NORM = 0.3989422804014327
BF = jnp.bfloat16
F32 = jnp.float32
GROUP = 16
CHANNELS = 64
COLUMNS = 32
DEPTH = 256
CAPACITY = 8
SLOT_TOTAL = 2048
POINTS = 1024
SCALING = 1.0 / math.sqrt(128 * 64 * 256)
VMEM_LIMIT = 56 * 1024 * 1024
ENC_CHUNK = 512
BLOCK_PAIRS = 1024


def frequencies():
    counted = np.arange(32)
    return np.where(counted < 16, counted, counted - 32)


def wave(length, positions, frequency):
    angles = 2.0 * np.pi * ((positions[:, None] * frequency[None, :]) % length) / length
    return np.cos(angles), np.sin(angles)


def bf16_of(array):
    return np.asarray(array, np.float32).astype(BF)


def kron_forward_y():
    cos, sin = wave(64, np.arange(64), frequencies())
    out = []
    for part in (cos, sin):
        w = part.reshape(16, 4, 16, 2)
        full = np.einsum("cjdp,ik->dpicjk", w, np.eye(8)).transpose(0, 1, 2, 3, 5, 4)
        out.append(full.reshape(256, 512))
    return bf16_of(np.concatenate(out))


def kron_forward_x():
    cos, sin = wave(128, np.arange(128), frequencies())
    out = []
    for part in (cos, sin):
        w = part.reshape(16, 8, 32)
        full = np.einsum("air,ps->rpasi", w, np.eye(2))
        out.append(full.reshape(64, 256))
    return bf16_of(np.concatenate(out))


def kron_inverse_x():
    cos, sin = wave(128, np.arange(128), frequencies())
    out = []
    for part in (cos, sin):
        w = part.reshape(16, 8, 32)
        full = np.einsum("air,ps->apirs", w, np.eye(2))
        out.append(full.reshape(256, 64))
    return bf16_of(np.concatenate(out))


def kron_inverse_y():
    cos, sin = wave(64, np.arange(64), frequencies())
    out = []
    for part in (cos, sin):
        w = part.reshape(16, 4, 16, 2)
        full = np.einsum("cjdp,ik->cijdpk", w, np.eye(8))
        out.append(full.reshape(512, 256))
    return bf16_of(np.concatenate(out))


def depth_waves():
    cos, sin = wave(256, np.arange(16), np.arange(256))
    return bf16_of(np.concatenate([cos, -sin]))


def entry_sums():
    return bf16_of(np.arange(2048)[:, None] // 8 == np.arange(256)[None, :])


def pair_sums():
    return bf16_of(np.arange(1024)[:, None] // 4 == np.arange(256)[None, :])


def nt(left, right):
    return lax.dot_general(left, right, (((1,), (1,)), ((), ())), preferred_element_type=F32)


def mm(left, right):
    return jnp.dot(left, right, preferred_element_type=F32)


def identity(n):
    rows = lax.broadcasted_iota(jnp.int32, (n, n), 0)
    lanes = lax.broadcasted_iota(jnp.int32, (n, n), 1)
    return jnp.where(rows == lanes, 1.0, 0.0).astype(BF)


def lane_sign(shape):
    lanes = lax.broadcasted_iota(jnp.int32, shape, 1)
    return jnp.where(lanes < CHANNELS, 1.0, -1.0)


def turned(cos_part, sin_part, direction):
    swapped = pltpu.roll(sin_part, CHANNELS, 1)
    return cos_part + swapped * (lane_sign(swapped.shape) * direction)


def greet():
    a, c = lax.axis_index("px"), lax.axis_index("py")
    barrier = pltpu.get_barrier_semaphore()

    def greeting(d, carry):
        pl.semaphore_signal(barrier, inc=1, device_id=((a + d) & 15, c), device_id_type=MESH)
        pl.semaphore_signal(barrier, inc=1, device_id=(a, (c + d) & 15), device_id_type=MESH)
        return carry

    lax.fori_loop(1, GROUP, greeting, 0)
    pl.semaphore_wait(barrier, 2 * (GROUP - 1))


def copy_to(axis, d, send, recv, send_sem, recv_sem):
    a, c = lax.axis_index("px"), lax.axis_index("py")
    me = a if axis == "px" else c
    peer = (me + d) & 15
    return pltpu.make_async_remote_copy(
        src_ref=send.at[peer],
        dst_ref=recv.at[me],
        send_sem=send_sem.at[d],
        recv_sem=recv_sem.at[me],
        device_id=(peer, c) if axis == "px" else (a, peer),
        device_id_type=MESH,
    )


def finish(axis, send, recv, send_sem, recv_sem):
    me = lax.axis_index(axis)
    recv[me] = send[me]

    def arrival(d, carry):
        copy_to(axis, d, send, recv, send_sem, recv_sem).wait_send()
        source = (me - d) & 15
        pltpu.make_async_remote_copy(
            src_ref=send.at[source],
            dst_ref=recv.at[source],
            send_sem=send_sem.at[d],
            recv_sem=recv_sem.at[source],
            device_id=(lax.axis_index("px"), lax.axis_index("py")),
            device_id_type=MESH,
        ).wait_recv()
        return carry

    lax.fori_loop(1, GROUP, arrival, 0)


def start_all(axis, send, recv, send_sem, recv_sem):
    def start(d, carry):
        copy_to(axis, d, send, recv, send_sem, recv_sem).start()
        return carry

    lax.fori_loop(1, GROUP, start, 0)


def exchange(axis, send, recv, send_sem, recv_sem):
    start_all(axis, send, recv, send_sem, recv_sem)
    finish(axis, send, recv, send_sem, recv_sem)


def sems():
    return [pltpu.SemaphoreType.DMA((GROUP,)), pltpu.SemaphoreType.DMA((GROUP,))]


def vmem(shape, kind):
    return pltpu.VMEM(shape, kind)


def whole():
    return pl.BlockSpec(memory_space=pltpu.VMEM)


def send_points_kernel(
    x_ref, route_ref, live_ref, out_ref,
    send1, recv1, send2, recv2, regroup, slot_ref, ss1, rs1, ss2, rs2,
):
    greet()
    live = live_ref[0]
    lanes = lax.broadcasted_iota(jnp.int32, (1, POINTS), 1)
    target = jnp.where(lanes < live, route_ref[...], 256)
    owners = lax.broadcasted_iota(jnp.int32, (256, POINTS), 0)
    named = jnp.where(owners == target, 1.0, 0.0)
    named_bf = named.astype(BF)
    rank = jnp.zeros((1, POINTS), F32)
    earlier = jnp.where(
        lax.broadcasted_iota(jnp.int32, (POINTS, POINTS), 0)
        < lax.broadcasted_iota(jnp.int32, (POINTS, POINTS), 1),
        1.0,
        0.0,
    ).astype(BF)
    counted = mm(named_bf, earlier)
    rank = jnp.sum(named * counted, axis=0, keepdims=True)
    slot_ref[...] = jnp.where(
        target < 256, target * CAPACITY + rank.astype(jnp.int32), -1
    )
    a = lax.axis_index("px")

    def pack(d, carry):
        peer = (a + d) & 15
        rows = lax.broadcasted_iota(jnp.int32, (128, POINTS), 0) + peer * 128
        hot = jnp.where(rows == slot_ref[...], 1.0, 0.0).astype(BF)
        send1[peer] = mm(hot, x_ref[...]).astype(BF)

        @pl.when(d > 0)
        def _():
            copy_to("px", d, send1, recv1, ss1, rs1).start()

        return carry

    lax.fori_loop(0, GROUP, pack, 0)
    finish("px", send1, recv1, ss1, rs1)
    for source in range(GROUP):
        regroup[source] = recv1[source].astype(F32).reshape(GROUP, CAPACITY, 128)
    for dest in range(GROUP):
        send2[dest] = regroup[:, dest].reshape(128, 128).astype(BF)
    exchange("py", send2, recv2, ss2, rs2)
    for source in range(GROUP):
        regroup[source] = recv2[source].astype(F32).reshape(GROUP, CAPACITY, 128)
    for source in range(GROUP):
        out_ref[source] = regroup[:, source].reshape(128, 128).astype(BF)


def send_points(x, route, live):
    block = (GROUP, 128, 128)
    return pl.pallas_call(
        send_points_kernel,
        out_shape=jax.ShapeDtypeStruct(block, BF),
        in_specs=[whole(), whole(), pl.BlockSpec(memory_space=pltpu.SMEM)],
        out_specs=whole(),
        scratch_shapes=[
            vmem(block, BF), vmem(block, BF), vmem(block, BF), vmem(block, BF),
            vmem((GROUP, GROUP, CAPACITY, 128), F32),
            vmem((1, POINTS), jnp.int32),
        ] + sems() + sems(),
        compiler_params=pltpu.CompilerParams(
            collective_id=0, has_side_effects=True, vmem_limit_bytes=VMEM_LIMIT
        ),
        name="send_points",
    )(x, route, live)


def encode_kernel(
    tab_ref, nbr_ref, cnt_ref, w1_ref, wo_ref, sums_ref, waves_ref,
    lat_ref, z_ref, extra_ref,
    table, pos_rows, high_ref, share_ref, prod, z_rows,
):
    eye = identity(128)
    picks = lax.broadcasted_iota(jnp.int32, (8, 128), 0)
    lanes8 = lax.broadcasted_iota(jnp.int32, (8, 128), 1)
    wanted = jnp.where(picks < 3, picks + 64, jnp.where(picks < 6, picks + 61, picks + 61))
    chooser = jnp.where(lanes8 == wanted, 1.0, 0.0).astype(BF)
    pos_rows[...] = jnp.zeros(pos_rows.shape, F32)
    for h in range(8):
        rows = tab_ref[h * 256 : (h + 1) * 256, :]
        turned_rows = nt(eye, rows)
        table[h * 64 : (h + 1) * 64, :] = turned_rows[0:64].astype(BF)
        extra = nt(chooser, rows)
        extra_ref[h] = extra
        for d in range(3):
            pos_rows[d * 8 + h : d * 8 + h + 1, :] = extra[d : d + 1]
    table[512:544, :] = pos_rows[...].astype(BF)
    counts = cnt_ref[...].astype(F32)
    share_ref[...] = 1.0 / counts
    spread = nt(counts.astype(BF), sums_ref[...])
    places = (lax.broadcasted_iota(jnp.int32, (COLUMNS, 2048), 1) & 7).astype(F32)
    high_ref[...] = jnp.where(places < spread, nbr_ref[...] >> 8, 8)
    n = ENC_CHUNK

    def column(ij, carry):
        cx = ((ij >> 2).astype(F32) + 0.5) * 0.25 - 1.0
        cy = ((ij & 3).astype(F32) + 0.5) * 0.5 - 1.0

        def chunk(step, inner):
            off = pl.multiple_of(step * n, n)
            low = nbr_ref[pl.ds(ij, 1), pl.ds(off, n)] & 255
            high = high_ref[pl.ds(ij, 1), pl.ds(off, n)]
            hot = jnp.where(
                lax.broadcasted_iota(jnp.int32, (256, n), 0) == low, 1.0, 0.0
            ).astype(BF)
            found = mm(table[...], hot)
            high8 = jnp.broadcast_to(high, (8, n))
            near = jnp.zeros((8, 8, n), F32)
            for h in range(8):
                part = found[h * 64 : (h + 1) * 64].reshape(8, 8, n)
                near = jnp.where((high8 == h)[None], part, near)
            sub = lax.broadcasted_iota(jnp.int32, (8, n), 0)
            place = found[512:536].reshape(3, 8, n)
            place = jnp.where((high8 == sub)[None], place, 0.0).reshape(24, n)
            depth = ((lax.broadcasted_iota(jnp.int32, (8, n), 1) + off) >> 3).astype(F32)
            cz = (depth + 0.5) * (2.0 / DEPTH) - 1.0
            part3 = jnp.where(sub >= 3, sub - 3, sub)
            centre = jnp.where(
                sub >= 6, 1.0, jnp.where(part3 == 0, cx, jnp.where(part3 == 1, cy, cz))
            )
            stacked = jnp.concatenate([place, place, centre], 0).astype(BF)
            half = mm(w1_ref[...], stacked)
            hidden = (half + half * jnp.tanh(half)).astype(BF)
            kernel = mm(wo_ref[...], hidden)
            prod[:, pl.ds(off, n)] = (kernel * near.reshape(64, n)).astype(BF)
            return inner

        lax.fori_loop(0, 2048 // n, chunk, 0)
        latent = mm(prod[...], sums_ref[...]) * share_ref[pl.ds(ij, 1), :]
        latent = latent.astype(BF)
        lat_ref[pl.ds(pl.multiple_of(ij * 64, 64), 64), :] = latent
        both = nt(waves_ref[...], latent)
        z_rows[:, pl.ds(ij, 1), :] = jnp.concatenate([both[0:16], both[16:32]], 1).reshape(
            16, 1, 128
        )
        return carry

    lax.fori_loop(0, COLUMNS, column, 0)
    z_ref[...] = z_rows[...].astype(BF)


def encode(tab, nbr, cnt, w1, wo):
    return pl.pallas_call(
        encode_kernel,
        out_shape=(
            jax.ShapeDtypeStruct((COLUMNS * 64, DEPTH), BF),
            jax.ShapeDtypeStruct((GROUP, COLUMNS, 128), BF),
            jax.ShapeDtypeStruct((8, 8, 256), F32),
        ),
        in_specs=[whole()] * 7,
        out_specs=(whole(),) * 3,
        scratch_shapes=[
            vmem((544, 256), BF),
            vmem((32, 256), F32),
            vmem((COLUMNS, 2048), jnp.int32),
            vmem((COLUMNS, DEPTH), F32),
            vmem((64, 2048), BF),
            vmem((GROUP, COLUMNS, 128), F32),
        ],
        compiler_params=pltpu.CompilerParams(vmem_limit_bytes=VMEM_LIMIT),
        name="encode",
    )(tab, nbr, cnt, w1, wo, jnp.asarray(entry_sums()), jnp.asarray(depth_waves()))


def forward_tail(z_ref, ky_ref, kx_ref, recv_a, send_b, recv_b, s1, r1, s2, r2):
    exchange("py", z_ref, recv_a, s1, r1)
    u = mm(ky_ref[...], recv_a[...].reshape(512, 128))
    send_b[...] = turned(u[:256], u[256:], 1.0).astype(BF).reshape(GROUP, 16, 128)
    exchange("px", send_b, recv_b, s2, r2)
    u = mm(kx_ref[...], recv_b[...].reshape(256, 128))
    return turned(u[:64], u[64:], 1.0) * SCALING


def own_doubling():
    return jnp.where(lax.axis_index("py") == 0, 1.0, 2.0)


def mixed(modes, weight_ref):
    lanes = lax.broadcasted_iota(jnp.int32, (64, 128), 1)
    swapped = pltpu.roll(modes, CHANNELS, 1)
    real2 = jnp.where(lanes < CHANNELS, modes, swapped)
    imag2 = jnp.where(lanes < CHANNELS, swapped, modes)
    rows4 = lax.broadcasted_iota(jnp.int32, (64, 256), 0) & 3
    keep = (lax.broadcasted_iota(jnp.int32, (64, 256), 1) >> 6) == rows4
    real4 = jnp.where(keep, jnp.concatenate([real2, real2], 1), 0.0)
    imag4 = jnp.where(keep, jnp.concatenate([imag2, imag2], 1), 0.0)
    first = (lax.broadcasted_iota(jnp.int32, (16, 128), 0) & 7) < 4
    out = []
    for h in range(8):
        left = jnp.concatenate([real4[8 * h : 8 * h + 8], imag4[8 * h : 8 * h + 8]], 0)
        left = left.astype(BF)
        lower = mm(left, weight_ref[8 * h : 8 * h + 4].reshape(256, 128))
        upper = mm(left, weight_ref[8 * h + 4 : 8 * h + 8].reshape(256, 128))
        both = jnp.where(first, lower, upper)
        out.append(turned(both[0:8], both[8:16], -1.0))
    return jnp.concatenate(out, 0)


def fourier_kernel(
    z_ref, weight_ref, ky_ref, kx_ref, kxi_ref, kyi_ref, modes_ref, back_ref,
    recv_a, send_b, recv_b, send_c, recv_c, send_d, recv_d,
    s1, r1, s2, r2, s3, r3, s4, r4,
):
    greet()
    modes = forward_tail(z_ref, ky_ref, kx_ref, recv_a, send_b, recv_b, s1, r1, s2, r2)
    modes_ref[...] = modes
    v = mixed(modes, weight_ref) * (own_doubling() * SCALING)
    u = mm(kxi_ref[...], v.astype(BF))
    send_c[...] = turned(u[:256], u[256:], -1.0).astype(BF).reshape(GROUP, 16, 128)
    exchange("px", send_c, recv_c, s3, r3)
    u = mm(kyi_ref[...], recv_c[...].reshape(256, 128))
    send_d[...] = turned(u[:512], u[512:], -1.0).astype(BF).reshape(GROUP, COLUMNS, 128)
    exchange("py", send_d, recv_d, s4, r4)
    back_ref[...] = recv_d[...]


def fourier(z, weight):
    wide, narrow = (GROUP, COLUMNS, 128), (GROUP, 16, 128)
    return pl.pallas_call(
        fourier_kernel,
        out_shape=(
            jax.ShapeDtypeStruct((64, 128), F32),
            jax.ShapeDtypeStruct(wide, BF),
        ),
        in_specs=[whole()] * 6,
        out_specs=(whole(),) * 2,
        scratch_shapes=[
            vmem(wide, BF), vmem(narrow, BF), vmem(narrow, BF), vmem(narrow, BF),
            vmem(narrow, BF), vmem(wide, BF), vmem(wide, BF),
        ] + sems() * 4,
        compiler_params=pltpu.CompilerParams(
            collective_id=1, has_side_effects=True, vmem_limit_bytes=VMEM_LIMIT
        ),
        name="fourier",
    )(
        z, weight, jnp.asarray(kron_forward_y()), jnp.asarray(kron_forward_x()),
        jnp.asarray(kron_inverse_x()), jnp.asarray(kron_inverse_y()),
    )


def gradient_modes_kernel(
    z_ref, ky_ref, kx_ref, modes_ref, recv_a, send_b, recv_b, s1, r1, s2, r2
):
    greet()
    modes = forward_tail(z_ref, ky_ref, kx_ref, recv_a, send_b, recv_b, s1, r1, s2, r2)
    modes_ref[...] = modes * own_doubling()


def gradient_modes(z):
    wide, narrow = (GROUP, COLUMNS, 128), (GROUP, 16, 128)
    return pl.pallas_call(
        gradient_modes_kernel,
        out_shape=jax.ShapeDtypeStruct((64, 128), F32),
        in_specs=[whole()] * 3,
        out_specs=whole(),
        scratch_shapes=[vmem(wide, BF), vmem(narrow, BF), vmem(narrow, BF)] + sems() * 2,
        compiler_params=pltpu.CompilerParams(
            collective_id=2, has_side_effects=True, vmem_limit_bytes=VMEM_LIMIT
        ),
        name="gradient_modes",
    )(z, jnp.asarray(kron_forward_y()), jnp.asarray(kron_forward_x()))


def split_rows(row, parts):
    sub = lax.broadcasted_iota(jnp.int32, (8, row.shape[1]), 0)
    out = jnp.zeros((8, row.shape[1]), F32)
    rest = row
    for part in range(parts):
        rounded = rest.astype(BF).astype(F32)
        out = jnp.where(sub == part, rounded, out)
        rest = rest - rounded
    return out.astype(BF)


def decode_kernel(
    lat_ref, back_ref, extra_ref, list_ref, w1_ref, wo_ref, skip_ref, read_ref,
    pairs_ref, waves_ref, pred_ref, z_ref,
    back_t, basis, latent_g, kern, total,
):
    flipped = nt(identity(128), back_ref[...].reshape(512, 128))
    back_t[...] = jnp.concatenate([flipped[0:64], flipped[64:128]], 1).astype(BF)
    total[...] = jnp.zeros(total.shape, F32)
    n = 256

    def block(h, carry):
        extras = extra_ref[h]
        expanded = nt(extras.astype(BF), pairs_ref[...])

        for step in range(BLOCK_PAIRS // n):
            off = step * n
            cells = list_ref[:, pl.ds(pl.multiple_of(h * BLOCK_PAIRS + off, n), n)]
            low, column = cells & 255, cells >> 8
            hot = jnp.where(
                lax.broadcasted_iota(jnp.int32, (256, n), 0) == low, 1.0, 0.0
            ).astype(BF)
            found = mm(lat_ref[...], hot)
            column8 = jnp.broadcast_to(column, (8, n))
            near = jnp.zeros((8, 8, n), F32)
            for k in range(COLUMNS):
                part = found[k * 64 : (k + 1) * 64].reshape(8, 8, n)
                near = jnp.where((column8 == k)[None], part, near)
            latent_g[:, off : off + n] = near.reshape(64, n).astype(BF)
            tw = mm(waves_ref[...], hot)
            match = lax.broadcasted_iota(jnp.int32, (COLUMNS, n), 0) == column
            for q in range(32):
                basis[q * 32 : (q + 1) * 32, off : off + n] = jnp.where(
                    match, tw[q : q + 1], 0.0
                ).astype(BF)
            sub = lax.broadcasted_iota(jnp.int32, (8, n), 0)
            cx = ((column >> 2).astype(F32) + 0.5) * 0.25 - 1.0
            cy = ((column & 3).astype(F32) + 0.5) * 0.5 - 1.0
            cz = (low.astype(F32) + 0.5) * (2.0 / DEPTH) - 1.0
            part3 = jnp.where(sub >= 3, sub - 3, sub)
            centre = jnp.where(
                sub >= 6, 1.0, jnp.where(part3 == 0, cx, jnp.where(part3 == 1, cy, cz))
            )
            stacked = jnp.concatenate([expanded[:, off : off + n], centre], 0).astype(BF)
            half = mm(w1_ref[...], stacked)
            hidden = (half + half * jnp.tanh(half)).astype(BF)
            kern[:, off : off + n] = mm(wo_ref[...], hidden)

        before = mm(back_t[...], basis[...]) + mm(skip_ref[...], latent_g[...])
        phi = 0.5 * (1.0 + lax.erf(before * HALF_ROOT))
        slope = phi + before * jnp.exp(-0.5 * before * before) * GAUSS_NORM
        weighed = kern[...] * read_ref[...]
        dots = jnp.sum(weighed * (before * phi), axis=0, keepdims=True)
        summed = jnp.sum(mm(split_rows(dots, 3), pairs_ref[...]), axis=0, keepdims=True)
        target, living = extras[6:7], extras[7:8]
        pred = living * (summed * 0.25)
        pred_ref[:, pl.ds(pl.multiple_of(h * 256, 256), 256)] = pred
        residue = living * (pred - target) * 0.25
        spread = jnp.sum(nt(split_rows(residue, 2), pairs_ref[...]), axis=0, keepdims=True)
        shares = (weighed * slope * spread).astype(BF)
        total[...] += nt(shares, basis[...])
        return carry

    lax.fori_loop(0, SLOT_TOTAL * 4 // BLOCK_PAIRS, block, 0)
    out = jnp.concatenate([total[:, 0:512].T, total[:, 512:1024].T], 1)
    z_ref[...] = out.astype(BF).reshape(GROUP, COLUMNS, 128)


def decode(lat, back, extra, lists, w1, wo, skip, readout):
    return pl.pallas_call(
        decode_kernel,
        out_shape=(
            jax.ShapeDtypeStruct((1, SLOT_TOTAL), F32),
            jax.ShapeDtypeStruct((GROUP, COLUMNS, 128), BF),
        ),
        in_specs=[whole()] * 10,
        out_specs=(whole(),) * 2,
        scratch_shapes=[
            vmem((64, 1024), BF),
            vmem((1024, BLOCK_PAIRS), BF),
            vmem((64, BLOCK_PAIRS), BF),
            vmem((64, BLOCK_PAIRS), F32),
            vmem((64, 1024), F32),
        ],
        compiler_params=pltpu.CompilerParams(vmem_limit_bytes=VMEM_LIMIT),
        name="decode",
    )(
        lat, back, extra, lists, w1, wo, skip, readout,
        jnp.asarray(pair_sums()), jnp.asarray(depth_waves()),
    )


def outer_kernel(modes_ref, grad_ref, out_ref):
    modes_t = modes_ref[...].T
    grads = grad_ref[...]
    swapped = pltpu.roll(grads, CHANNELS, 1) * lane_sign(grads.shape)
    for m in range(8):
        out_ref[m] = (
            modes_t[0:64, m : m + 1] * grads[m : m + 1]
            + modes_t[64:128, m : m + 1] * swapped[m : m + 1]
        )


def outer(modes, grads):
    return pl.pallas_call(
        outer_kernel,
        grid=(8,),
        out_shape=jax.ShapeDtypeStruct((64, 64, 128), F32),
        in_specs=[pl.BlockSpec((8, 128), lambda i: (i, 0))] * 2,
        out_specs=pl.BlockSpec((8, 64, 128), lambda i: (i, 0, 0)),
        compiler_params=pltpu.CompilerParams(vmem_limit_bytes=VMEM_LIMIT),
        name="outer",
    )(modes, grads)


def two_parts(values):
    high = lax.reduce_precision(values, 8, 7)
    return high.astype(BF), (values - high).astype(BF)


def encoder_first(weight, bias):
    high, low = two_parts(weight * 0.5)
    bias_high, bias_low = two_parts(bias * 0.5)
    return jnp.concatenate(
        [
            jnp.repeat(high, 8, axis=0), jnp.repeat(low, 8, axis=0),
            -high, -low, bias_high[None], bias_low[None],
        ],
        0,
    ).T


def decoder_first(weight, bias):
    high, low = two_parts(weight * 0.5)
    bias_high, bias_low = two_parts(bias * 0.5)
    return jnp.concatenate(
        [
            high, low, jnp.zeros((2, weight.shape[1]), BF),
            -high, -low, bias_high[None], bias_low[None],
        ],
        0,
    ).T


def body(
    point_features, positions, targets, routes, live_counts, cell_neighbours, cell_counts,
    slot_neighbours, encoder_in, encoder_bias, encoder_out, decoder_in, decoder_bias,
    decoder_out, skip_weight, spectral_weight, readout_weight,
):
    x = jnp.concatenate(
        [
            point_features, positions, targets[:, None],
            jnp.ones((POINTS, 1), BF), jnp.zeros((POINTS, 59), BF),
        ],
        1,
    )
    tab = send_points(x, routes.reshape(1, POINTS), live_counts)
    lat, z, extra = encode(
        tab.reshape(SLOT_TOTAL, 128),
        cell_neighbours.reshape(COLUMNS, 2048),
        cell_counts.reshape(COLUMNS, DEPTH),
        encoder_first(encoder_in, encoder_bias),
        encoder_out.T,
    )
    modes, back = fourier(z, spectral_weight.reshape(64, 64, 128))
    pred, grad_z = decode(
        lat, back, extra, slot_neighbours,
        decoder_first(decoder_in, decoder_bias), decoder_out.T, skip_weight.T,
        readout_weight[:, None],
    )
    grads = gradient_modes(grad_z)
    return pred, outer(modes, grads).reshape(32, 2, 1, 64, 128)


def solution(mesh):
    in_specs = (
        P(("px", "py"), None), P(("px", "py"), None), P(("px", "py")), P(("px", "py"), None),
        P(("px", "py")), P("px", "py", None), P("px", "py", None), P(("px", "py"), None),
        P(), P(), P(), P(), P(), P(), P(),
        P(None, "px", "py", None, None), P(),
    )
    out_specs = (P(("px", "py"), None), P(None, "px", "py", None, None))
    return jax.shard_map(body, mesh=mesh, in_specs=in_specs, out_specs=out_specs, check_vma=False)
```

time: 1010 us -> 229 us (0.23)
  local copies, waits for them, and re-layouts: 671 us -> 9.37 us
  Pallas kernels: 0 us -> 218 us
  other arithmetic: 152 us -> 0.04 us
  matrix products: 58 us -> 0 us
  waiting for transfers between devices: 55.5 us -> 0 us
  starting transfers between devices: 46.8 us -> 0 us
  blocking collectives: 15.9 us -> 0 us
    gather x42 -> x0, local copies, waits for them, and re-layouts: 511 us -> none  [the longest x16 205 us: encode_cells(): nearby = slot_features[flat_ids]]
    pallas_call x0 -> x6, Pallas kernels: none -> 218 us  [the longest x1 97.1 us: encode(): pl.pallas_call(encode_kernel, out_shape=(jax.ShapeDtypeStruct((COLUMNS *...]
    reduce_sum x12 -> x0, other arithmetic: 61.6 us -> none  [the longest x8 55.6 us: encode_cells(): summed = jnp.sum(jnp.where(kept_mask[:, :, None], summands, 0.0), axis=1)]
    dot_general x45 -> x0, matrix products: 58 us -> none  [the longest x30 22.1 us: contract(): return jnp.einsum(form, left, right, precision=PRECISE)]
    all_to_all x9 -> x0, waiting for transfers between devices: 55.5 us -> none  [the longest x2 14.4 us: forward_modes(): lax.all_to_all(jnp.concatenate([y_real, y_imag], 3), 'px', split_axis=1,...]
    slice x14 -> x0, local copies, waits for them, and re-layouts: 49.7 us -> none  [the longest x10 49.4 us: kernel_hidden(): offset[:, 0:1] * weight_in[0] + offset[:, 1:2] * weight_in[1]]
    scatter-add x2 -> x0, other arithmetic: 49.1 us -> none  [decode_step(): jax.ops.segment_sum(shares, block_lists.reshape(-1), num_segments=cell_to...]
    all_to_all x9 -> x0, starting transfers between devices: 46.8 us -> none  [the longest x1 11.1 us: body(): lax.all_to_all(lax.all_to_all(side_data, 'px', split_axis=0, concat_axis=...]
  transfers between devices with their start and end apart: 9 -> 0, of which waited for: 9 -> 0; matrix products, arithmetic and copies ran while one was open for 2% -> 0% of each run, Pallas kernels for 0% -> 0%
where the time goes in v1:
time: 229 us; the launch traced here: 228 us
  Pallas kernels  218 us (95%)
  local copies, waits for them, and re-layouts  9.37 us (4%)
    pallas_call x1, Pallas kernels, encode(): pl.pallas_call(encode_kernel, out_shape=(jax.ShapeDtypeStruct((COLUMNS *...  97.1 us
    pallas_call x1, Pallas kernels, send_points(): pl.pallas_call(send_points_kernel, out_shape=jax.ShapeDtypeStruct(block,...  36.3 us
    pallas_call x1, Pallas kernels, fourier(): pl.pallas_call(fourier_kernel, out_shape=(jax.ShapeDtypeStruct((64, 128),...  31.3 us
    pallas_call x1, Pallas kernels, decode(): pl.pallas_call(decode_kernel, out_shape=(jax.ShapeDtypeStruct((1, SLOT_TO...  30.9 us
    pallas_call x1, Pallas kernels, gradient_modes(): pl.pallas_call(gradient_modes_kernel, out_shape=jax.ShapeDtypeStruct((64,...  16.5 us
    pallas_call x1, Pallas kernels, outer(): pl.pallas_call(outer_kernel, grid=(8,), out_shape=jax.ShapeDtypeStruct((6...  5.51 us

profile of v1, /device:TPU:1, one launch (start us, length us, event | category | flops | bytes accessed | tf_op | source)
XLA Modules:
  0.0 228.4 jit_solution(17285114284906317366)
XLA Ops:
  0.6 0.0 copy-start
  0.6 0.0 copy-start.1
  0.6 1.1 copy.78
  1.8 0.0 copy-start.4
  1.8 0.0 copy-start.7
  1.8 0.9 copy.79
  2.7 0.9 broadcast_in_dim.44
  3.7 1.3 concatenate.9.x_ref
  5.6 36.3 %send_points.1 = bf16[16,128,128]{2,1,0:T(8,128)(2,1)} custom-call(bf16[1024,128]{1,0:T(8,128)(2,1)} %concatenate.9.x_ref, s32[1,1024]{1,0:T(1,128)} %bitcast.28, s32[1]{0:T(128)S(6)} %copy.93.live_ref), custom_call_target="tpu_custom_call" | custom-call | tf_op jit(solution)/shard_map/send_points/pallas_call | solution.py:245
  41.9 0.0 copy-done
  41.9 0.8 reshape.30.nbr_ref
  42.7 0.0 copy-done.1
  42.7 0.6 reshape.31.cnt_ref
  43.4 0.0 copy-done.4
  43.4 0.1 copy.81
  43.5 0.1 copy.82
  43.6 0.1 copy.85
  43.7 0.1 copy.84
  43.8 0.1 copy.86
  43.9 0.0 copy-done.7
  43.9 0.1 copy.87
  44.0 0.1 copy.88
  44.2 0.7 concatenate.10
  44.9 97.1 %encode.1 = (bf16[2048,256]{1,0:T(8,128)(2,1)}, bf16[16,32,128]{2,1,0:T(8,128)(2,1)}, f32[8,8,256]{2,1,0:T(8,128)}) custom-call(bf16[2048,128]{1,0:T(8,128)(2,1)} %bitcast.21, s32[32,2048]{1,0:T(8,128)} %reshape.30.nbr_ref, s32[32,256]{1,0:T(8,128)} %reshape.31.cnt_ref, bf16[80,56]{1,0:T(8,128)(2,1)} %bitcast.24, bf16[64,80]{1,0:T(8,128)(2,1)} %bitcast.27, ...), custom_call_target="tpu_custom_call" | custom-call | tf_op jit(solution)/shard_map/encode/pallas_call | solution.py:337
  142.0 31.3 %fourier.1 = (f32[64,128]{1,0:T(8,128)}, bf16[16,32,128]{2,1,0:T(8,128)(2,1)}) custom-call(bf16[16,32,128]{2,1,0:T(8,128)(2,1)} %get-tuple-element.10.z_ref, bf16[64,64,128]{2,1,0:T(8,128)(2,1)} %bitcast.22, bf16[512,512]{1,0:T(8,128)(2,1)} %constant.8.clone.ky_ref, bf16[128,256]{1,0:T(8,128)(2,1)} %constant.9.clone.kx_ref, ...), custom_call_target="tpu_custom_call" | custom-call | tf_op jit(solution)/shard_map/fourier/pallas_call | solution.py:413
  173.4 0.7 copy.89
  174.2 0.7 copy.90
  174.8 0.0 copy-done.6
  174.8 0.7 copy.91.read_ref
  175.6 30.9 %decode.1 = (f32[1,2048]{1,0:T(1,128)}, bf16[16,32,128]{2,1,0:T(8,128)(2,1)}) custom-call(bf16[2048,256]{1,0:T(8,128)(2,1)} %get-tuple-element.9.lat_ref, bf16[16,32,128]{2,1,0:T(8,128)(2,1)} %get-tuple-element.11.back_ref, f32[8,8,256]{2,1,0:T(8,128)} %get-tuple-element.12.extra_ref, s32[1,8192]{1,0:T(1,128)} %list_ref.1, bf16[256,16]{1,0:T(8,128)(2,1)} %bitcast.23, ...), custom_call_target="tpu_custom_call" | custom-call | tf_op jit(solution)/shard_map/decode/pallas_call | solution.py:537
  206.5 16.5 %gradient_modes.1.grad_ref = f32[64,128]{1,0:T(8,128)} custom-call(bf16[16,32,128]{2,1,0:T(8,128)(2,1)} %get-tuple-element.15.z_ref, bf16[512,512]{1,0:T(8,128)(2,1)} %constant.8.clone.ky_ref, bf16[128,256]{1,0:T(8,128)(2,1)} %constant.9.clone.kx_ref), custom_call_target="tpu_custom_call" | custom-call | tf_op jit(solution)/shard_map/gradient_modes/pallas_call | solution.py:445
  222.9 5.5 %outer.1 = f32[64,64,128]{2,1,0:T(8,128)} custom-call(f32[64,128]{1,0:T(8,128)} %get-tuple-element.14.modes_ref, f32[64,128]{1,0:T(8,128)} %gradient_modes.1.grad_ref), custom_call_target="tpu_custom_call" | custom-call | tf_op jit(solution)/shard_map/outer/pallas_call | solution.py:572
  (20 shorter events, 0.2 us)
Async XLA Ops:
  0.6 41.3 %copy-start = (s32[8,4,2048]{2,1,0:T(4,128)S(1)}, s32[8,4,2048]{2,1,0:T(4,128)}, u32[]{:S(2)}) copy-start(s32[8,4,2048]{2,1,0:T(4,128)} %param.32) | copy-start | bytes 786436
  0.6 42.1 %copy-start.1 = (s32[8,4,256]{2,1,0:T(4,128)S(1)}, s32[8,4,256]{2,1,0:T(4,128)}, u32[]{:S(2)}) copy-start(s32[8,4,256]{2,1,0:T(4,128)} %param.33) | copy-start | bytes 98308
  1.8 41.6 %copy-start.4 = (f32[3,80]{1,0:T(4,128)S(1)}, f32[3,80]{1,0:T(4,128)}, u32[]{:S(2)}) copy-start(f32[3,80]{1,0:T(4,128)} %param.35) | copy-start | bytes 2884
  1.8 42.1 %copy-start.7 = (f32[80]{0:T(128)S(1)}, f32[80]{0:T(128)}, u32[]{:S(2)}) copy-start(f32[80]{0:T(128)} %param.36) | copy-start | bytes 964
  44.9 128.4 %copy-start.3 = (f32[3,256]{1,0:T(4,128)S(1)}, f32[3,256]{1,0:T(4,128)}, u32[]{:S(2)}) copy-start(f32[3,256]{1,0:T(4,128)} %param.38) | copy-start | bytes 9220
  44.9 128.4 %copy-start.5 = (f32[256]{0:T(256)S(1)}, f32[256]{0:T(256)}, u32[]{:S(2)}) copy-start(f32[256]{0:T(256)} %param.39) | copy-start | bytes 3076
  44.9 129.3 %copy-start.2 = (bf16[64,64]{1,0:T(8,128)(2,1)S(1)}, bf16[64,64]{1,0:T(8,128)(2,1)}, u32[]{:S(2)}) copy-start(bf16[64,64]{1,0:T(8,128)(2,1)} %param.41) | copy-start | bytes 24580
  44.9 130.0 %copy-start.6 = (f32[64]{0:T(128)S(1)}, f32[64]{0:T(128)}, u32[]{:S(2)}) copy-start(f32[64]{0:T(128)} %param.43) | copy-start | bytes 772

commit v2 on v1

v2 whole, which is shorter than its diff:
```python
import math
import types

import jax
import jax.numpy as jnp
import numpy as np
from jax import lax
from jax.experimental import pallas as pl
from jax.experimental.pallas import tpu as pltpu
from jax.sharding import PartitionSpec as P

MESH = pl.DeviceIdType.MESH
HALF_ROOT = 0.7071067811865476
GAUSS_NORM = 0.3989422804014327
BF = jnp.bfloat16
F32 = jnp.float32
GROUP = 16
CHANNELS = 64
COLUMNS = 32
DEPTH = 256
CAPACITY = 8
SLOT_TOTAL = 2048
POINTS = 1024
SCALING = 1.0 / math.sqrt(128 * 64 * 256)
VMEM_LIMIT = 60 * 1024 * 1024
ENC_COLUMNS = 2
PREP = 512
POST = 2048


def frequencies():
    counted = np.arange(32)
    return np.where(counted < 16, counted, counted - 32)


def wave(length, positions, frequency):
    angles = 2.0 * np.pi * ((positions[:, None] * frequency[None, :]) % length) / length
    return np.cos(angles), np.sin(angles)


def bf16_of(array):
    return np.asarray(array, np.float32).astype(BF)


def kron_forward_y():
    cos, sin = wave(64, np.arange(64), frequencies())
    out = []
    for part in (cos, sin):
        w = part.reshape(16, 4, 16, 2)
        full = np.einsum("cjdp,ik->dpicjk", w, np.eye(8)).transpose(0, 1, 2, 3, 5, 4)
        out.append(full.reshape(256, 512))
    return bf16_of(np.concatenate(out))


def kron_forward_x():
    cos, sin = wave(128, np.arange(128), frequencies())
    out = []
    for part in (cos, sin):
        w = part.reshape(16, 8, 32)
        full = np.einsum("air,ps->rpasi", w, np.eye(2))
        out.append(full.reshape(64, 256))
    return bf16_of(np.concatenate(out))


def kron_inverse_x():
    cos, sin = wave(128, np.arange(128), frequencies())
    out = []
    for part in (cos, sin):
        w = part.reshape(16, 8, 32)
        full = np.einsum("air,ps->apirs", w, np.eye(2))
        out.append(full.reshape(256, 64))
    return bf16_of(np.concatenate(out))


def kron_inverse_y():
    cos, sin = wave(64, np.arange(64), frequencies())
    out = []
    for part in (cos, sin):
        w = part.reshape(16, 4, 16, 2)
        full = np.einsum("cjdp,ik->cijdpk", w, np.eye(8))
        out.append(full.reshape(512, 256))
    return bf16_of(np.concatenate(out))


def depth_waves():
    cos, sin = wave(256, np.arange(16), np.arange(256))
    return bf16_of(np.concatenate([cos, -sin]))


def entry_sums():
    return bf16_of(np.arange(2048)[:, None] // 8 == np.arange(256)[None, :])


def pair_sums():
    return bf16_of(np.arange(1024)[:, None] // 4 == np.arange(256)[None, :])


def nt(left, right):
    return lax.dot_general(left, right, (((1,), (1,)), ((), ())), preferred_element_type=F32)


def mm(left, right):
    return jnp.dot(left, right, preferred_element_type=F32)


def identity(n):
    rows = lax.broadcasted_iota(jnp.int32, (n, n), 0)
    lanes = lax.broadcasted_iota(jnp.int32, (n, n), 1)
    return jnp.where(rows == lanes, 1.0, 0.0).astype(BF)


def lane_sign(shape):
    lanes = lax.broadcasted_iota(jnp.int32, shape, 1)
    return jnp.where(lanes < CHANNELS, 1.0, -1.0)


def turned(cos_part, sin_part, direction):
    swapped = pltpu.roll(sin_part, CHANNELS, 1)
    return cos_part + swapped * (lane_sign(swapped.shape) * direction)


def others():
    a, c = lax.axis_index("px"), lax.axis_index("py")
    return a, c


def greet():
    a, c = others()
    barrier = pltpu.get_barrier_semaphore()

    def greeting(d, carry):
        pl.semaphore_signal(barrier, inc=1, device_id=((a + d) & 15, c), device_id_type=MESH)
        pl.semaphore_signal(barrier, inc=1, device_id=(a, (c + d) & 15), device_id_type=MESH)
        return carry

    lax.fori_loop(1, GROUP, greeting, 0)


def greeted():
    pl.semaphore_wait(pltpu.get_barrier_semaphore(), 2 * (GROUP - 1))


def copy_to(axis, d, send, recv, send_sem, recv_sem):
    a, c = others()
    me = a if axis == "px" else c
    peer = (me + d) & 15
    return pltpu.make_async_remote_copy(
        src_ref=send.at[peer],
        dst_ref=recv.at[me],
        send_sem=send_sem.at[d],
        recv_sem=recv_sem.at[me],
        device_id=(peer, c) if axis == "px" else (a, peer),
        device_id_type=MESH,
    )


def start_all(axis, send, recv, send_sem, recv_sem):
    def start(d, carry):
        copy_to(axis, d, send, recv, send_sem, recv_sem).start()
        return carry

    lax.fori_loop(1, GROUP, start, 0)


def finish(axis, send, recv, send_sem, recv_sem):
    me = lax.axis_index(axis)
    recv[me] = send[me]

    def arrival(d, carry):
        copy_to(axis, d, send, recv, send_sem, recv_sem).wait_send()
        source = (me - d) & 15
        pltpu.make_async_remote_copy(
            src_ref=send.at[source],
            dst_ref=recv.at[source],
            send_sem=send_sem.at[d],
            recv_sem=recv_sem.at[source],
            device_id=others(),
            device_id_type=MESH,
        ).wait_recv()
        return carry

    lax.fori_loop(1, GROUP, arrival, 0)


def exchange(axis, send, recv, pair, meanwhile=None):
    start_all(axis, send, recv, *pair)
    if meanwhile is not None:
        meanwhile()
    finish(axis, send, recv, *pair)


def send_points(r):
    greet()
    live = r.live[0]
    lanes = lax.broadcasted_iota(jnp.int32, (1, POINTS), 1)
    target = jnp.where(lanes < live, r.route[...], 256)
    owners = lax.broadcasted_iota(jnp.int32, (256, POINTS), 0)
    named = jnp.where(owners == target, 1.0, 0.0)
    earlier = jnp.where(
        lax.broadcasted_iota(jnp.int32, (POINTS, POINTS), 0)
        < lax.broadcasted_iota(jnp.int32, (POINTS, POINTS), 1),
        1.0,
        0.0,
    ).astype(BF)
    counted = mm(named.astype(BF), earlier)
    rank = jnp.sum(named * counted, axis=0, keepdims=True)
    r.slot[...] = jnp.where(target < 256, target * CAPACITY + rank.astype(jnp.int32), -1)
    greeted()
    a = lax.axis_index("px")

    def pack(d, carry):
        peer = (a + d) & 15
        rows = lax.broadcasted_iota(jnp.int32, (128, POINTS), 0) + peer * 128
        hot = jnp.where(rows == r.slot[...], 1.0, 0.0).astype(BF)
        r.send1[peer] = mm(hot, r.x[...]).astype(BF)

        @pl.when(d > 0)
        def _():
            copy_to("px", d, r.send1, r.recv1, r.s1, r.r1).start()

        return carry

    lax.fori_loop(0, GROUP, pack, 0)
    finish("px", r.send1, r.recv1, r.s1, r.r1)
    for source in range(GROUP):
        r.regroup[source] = r.recv1[source].astype(F32).reshape(GROUP, CAPACITY, 128)
    for dest in range(GROUP):
        r.send2[dest] = r.regroup[:, dest].reshape(128, 128).astype(BF)
    exchange("py", r.send2, r.recv2, (r.s2, r.r2))
    for source in range(GROUP):
        r.regroup[source] = r.recv2[source].astype(F32).reshape(GROUP, CAPACITY, 128)
    for source in range(GROUP):
        r.tab[source * 128 : (source + 1) * 128, :] = (
            r.regroup[:, source].reshape(128, 128).astype(BF)
        )


def first_layer_centres(ij, depth, sub):
    cx = ((ij >> 2).astype(F32) + 0.5) * 0.25 - 1.0
    cy = ((ij & 3).astype(F32) + 0.5) * 0.5 - 1.0
    cz = (depth.astype(F32) + 0.5) * (2.0 / DEPTH) - 1.0
    part3 = jnp.where(sub >= 3, sub - 3, sub)
    return jnp.where(
        sub >= 6, 1.0, jnp.where(part3 == 0, cx, jnp.where(part3 == 1, cy, cz))
    )


def encode(r):
    eye = identity(128)
    picks = lax.broadcasted_iota(jnp.int32, (8, 128), 0)
    lanes8 = lax.broadcasted_iota(jnp.int32, (8, 128), 1)
    wanted = jnp.where(picks < 3, picks + 64, picks + 61)
    chooser = jnp.where(lanes8 == wanted, 1.0, 0.0).astype(BF)
    r.pos_rows[...] = jnp.zeros(r.pos_rows.shape, F32)
    for h in range(8):
        rows = r.tab[h * 256 : (h + 1) * 256, :]
        r.table[h * 64 : (h + 1) * 64, :] = nt(eye, rows)[0:64].astype(BF)
        extra = nt(chooser, rows)
        r.extra[h] = extra
        r.target[h : h + 1, :] = extra[6:7]
        r.living[h : h + 1, :] = extra[7:8]
        for d in range(3):
            r.pos_rows[d * 8 + h : d * 8 + h + 1, :] = extra[d : d + 1]
    r.table[512:544, :] = r.pos_rows[...].astype(BF)
    counts = r.cnt[...].astype(F32)
    steps = COLUMNS // ENC_COLUMNS
    places = (lax.broadcasted_iota(jnp.int32, (steps, 2048), 1) & 7).astype(F32)
    for k in range(ENC_COLUMNS):
        spread = nt(counts[:, k * DEPTH : (k + 1) * DEPTH].astype(BF), r.sums[...])
        ids = r.nbr[:, k * 2048 : (k + 1) * 2048]
        r.high[:, k * 2048 : (k + 1) * 2048] = jnp.where(places < spread, ids >> 8, 8)
    n = 2048 * ENC_COLUMNS

    def columns(step, carry):
        low = r.nbr[pl.ds(step, 1), :] & 255
        high = r.high[pl.ds(step, 1), :]
        hot = jnp.where(
            lax.broadcasted_iota(jnp.int32, (256, n), 0) == low, 1.0, 0.0
        ).astype(BF)
        found = mm(r.table[...], hot)
        high8 = jnp.broadcast_to(high, (8, n))
        near = jnp.zeros((8, 8, n), F32)
        for h in range(8):
            part = found[h * 64 : (h + 1) * 64].reshape(8, 8, n)
            near = jnp.where((high8 == h)[None], part, near)
        sub = lax.broadcasted_iota(jnp.int32, (8, n), 0)
        lane = lax.broadcasted_iota(jnp.int32, (8, n), 1)
        place = found[512:536].reshape(3, 8, n)
        place = jnp.where((high8 == sub)[None], place, 0.0).reshape(24, n)
        ij = (lane >> 11) + step * ENC_COLUMNS
        centre = first_layer_centres(ij, (lane & 2047) >> 3, sub)
        stacked = jnp.concatenate([place, place, centre], 0).astype(BF)
        half = mm(r.ew1[...], stacked)
        hidden = (half + half * jnp.tanh(half)).astype(BF)
        kernel = mm(r.ewo[...], hidden)
        shares = (kernel * near.reshape(64, n)).astype(BF)
        for k in range(ENC_COLUMNS):
            row = pl.multiple_of((step * ENC_COLUMNS + k) * 64, 64)
            r.prod[pl.ds(row, 64), :] = shares[:, k * 2048 : (k + 1) * 2048]
        return carry

    lax.fori_loop(0, steps, columns, 0)
    shares = 1.0 / counts
    group = 8
    for g in range(COLUMNS // group):
        latent = mm(r.prod[g * group * 64 : (g + 1) * group * 64, :], r.sums[...])
        for k in range(group):
            ij = g * group + k
            row, part = ij // ENC_COLUMNS, ij % ENC_COLUMNS
            share = shares[row : row + 1, part * DEPTH : (part + 1) * DEPTH]
            r.lat[ij * 64 : (ij + 1) * 64, :] = (
                latent[k * 64 : (k + 1) * 64] * share
            ).astype(BF)
    both = nt(r.waves[...], r.lat[...])
    for ij in range(COLUMNS):
        part = both[:, ij * 64 : (ij + 1) * 64]
        r.z_rows[:, ij : ij + 1, :] = jnp.concatenate([part[0:16], part[16:32]], 1).reshape(
            16, 1, 128
        )
    r.z[...] = r.z_rows[...].astype(BF)


def forward_modes(z, r, pairs, recv_a, send_b, recv_b, meanwhile):
    exchange("py", z, recv_a, pairs[0], meanwhile(0))
    u = mm(r.ky[...], recv_a[...].reshape(512, 128))
    send_b[...] = turned(u[:256], u[256:], 1.0).astype(BF).reshape(GROUP, 16, 128)
    exchange("px", send_b, recv_b, pairs[1], meanwhile(1))
    u = mm(r.kx[...], recv_b[...].reshape(256, 128))
    return turned(u[:64], u[64:], 1.0) * SCALING


def own_doubling():
    return jnp.where(lax.axis_index("py") == 0, 1.0, 2.0)


def mixed(modes, weight_ref):
    lanes = lax.broadcasted_iota(jnp.int32, (64, 128), 1)
    swapped = pltpu.roll(modes, CHANNELS, 1)
    real2 = jnp.where(lanes < CHANNELS, modes, swapped)
    imag2 = jnp.where(lanes < CHANNELS, swapped, modes)
    rows4 = lax.broadcasted_iota(jnp.int32, (64, 256), 0) & 3
    keep = (lax.broadcasted_iota(jnp.int32, (64, 256), 1) >> 6) == rows4
    real4 = jnp.where(keep, jnp.concatenate([real2, real2], 1), 0.0)
    imag4 = jnp.where(keep, jnp.concatenate([imag2, imag2], 1), 0.0)
    first = (lax.broadcasted_iota(jnp.int32, (16, 128), 0) & 7) < 4
    out = []
    for h in range(8):
        left = jnp.concatenate([real4[8 * h : 8 * h + 8], imag4[8 * h : 8 * h + 8]], 0)
        left = left.astype(BF)
        lower = mm(left, weight_ref[8 * h : 8 * h + 4].reshape(256, 128))
        upper = mm(left, weight_ref[8 * h + 4 : 8 * h + 8].reshape(256, 128))
        both = jnp.where(first, lower, upper)
        out.append(turned(both[0:8], both[8:16], -1.0))
    return jnp.concatenate(out, 0)


def fourier(r, meanwhile):
    modes = forward_modes(
        r.z, r, ((r.s3, r.r3), (r.s4, r.r4)), r.recv_a, r.send_b, r.recv_b, meanwhile
    )
    r.modes[...] = modes
    v = mixed(modes, r.weight) * (own_doubling() * SCALING)
    u = mm(r.kxi[...], v.astype(BF))
    r.send_c[...] = turned(u[:256], u[256:], -1.0).astype(BF).reshape(GROUP, 16, 128)
    exchange("px", r.send_c, r.recv_c, (r.s5, r.r5), meanwhile(2))
    u = mm(r.kyi[...], r.recv_c[...].reshape(256, 128))
    r.send_d[...] = turned(u[:512], u[512:], -1.0).astype(BF).reshape(GROUP, COLUMNS, 128)
    exchange("py", r.send_d, r.recv_d, (r.s6, r.r6), meanwhile(3))


def prepare(r, first, last):
    n = PREP

    def block(step, carry):
        off = pl.multiple_of(step * n, n)
        half_block = step & 1
        expanded = nt(
            r.extra[step >> 1].astype(BF),
            r.pairs[pl.ds(pl.multiple_of(half_block * n, n), n), :],
        )
        cells = r.lists[:, pl.ds(off, n)]
        low, column = cells & 255, cells >> 8
        hot = jnp.where(
            lax.broadcasted_iota(jnp.int32, (256, n), 0) == low, 1.0, 0.0
        ).astype(BF)
        found = mm(r.lat[...], hot)
        column8 = jnp.broadcast_to(column, (8, n))
        near = jnp.zeros((8, 8, n), F32)
        for k in range(COLUMNS):
            part = found[k * 64 : (k + 1) * 64].reshape(8, 8, n)
            near = jnp.where((column8 == k)[None], part, near)
        r.before[:, pl.ds(off, n)] = mm(r.skip[...], near.reshape(64, n).astype(BF))
        tw = mm(r.waves[...], hot)
        match = lax.broadcasted_iota(jnp.int32, (COLUMNS, n), 0) == column
        for q in range(32):
            r.basis[q * 32 : (q + 1) * 32, pl.ds(off, n)] = jnp.where(
                match, tw[q : q + 1], 0.0
            ).astype(BF)
        sub = lax.broadcasted_iota(jnp.int32, (8, n), 0)
        stacked = jnp.concatenate(
            [expanded, first_layer_centres(column, low, sub)], 0
        ).astype(BF)
        half = mm(r.dw1[...], stacked)
        hidden = (half + half * jnp.tanh(half)).astype(BF)
        r.kern[:, pl.ds(off, n)] = mm(r.dwo[...], hidden) * r.read[...]
        return carry

    lax.fori_loop(first, last, block, 0)


def parts_of(values, parts):
    out, rest = [], values
    for _ in range(parts):
        rounded = rest.astype(BF).astype(F32)
        out.append(rounded)
        rest = rest - rounded
    return jnp.concatenate(out, 0).astype(BF)


def decode(r):
    flipped = nt(identity(128), r.recv_d[...].reshape(512, 128))
    r.back_t[...] = jnp.concatenate([flipped[0:64], flipped[64:128]], 1).astype(BF)
    n = POST

    def forward(step, carry):
        off = pl.multiple_of(step * n, n)
        here = pl.ds(off, n)
        before = mm(r.back_t[...], r.basis[:, here]) + r.before[:, here]
        phi = 0.5 * (1.0 + lax.erf(before * HALF_ROOT))
        slope = phi + before * jnp.exp(-0.5 * before * before) * GAUSS_NORM
        weighed = r.kern[:, here]
        r.kern[:, here] = weighed * slope
        dots = jnp.sum(weighed * (before * phi), axis=0, keepdims=True)
        for k in range(n // 1024):
            r.dots[pl.ds(step * (n // 1024) + k, 1), :] = dots[:, k * 1024 : (k + 1) * 1024]
        return carry

    lax.fori_loop(0, 4 * SLOT_TOTAL // n, forward, 0)
    summed = mm(parts_of(r.dots[...], 3), r.pairs[...])
    summed = summed[0:8] + summed[8:16] + summed[16:24]
    living = r.living[...]
    pred = living * (summed * 0.25)
    for h in range(8):
        r.pred[:, h * 256 : (h + 1) * 256] = pred[h : h + 1]
    residue = living * (pred - r.target[...]) * 0.25
    spread = nt(parts_of(residue, 2), r.pairs[...])
    r.dots[...] = spread[0:8] + spread[8:16]
    r.total[...] = jnp.zeros(r.total.shape, F32)

    def backward(step, carry):
        here = pl.ds(pl.multiple_of(step * 1024, 1024), 1024)
        shares = (r.kern[:, here] * r.dots[pl.ds(step, 1), :]).astype(BF)
        r.total[...] += nt(shares, r.basis[:, here])
        return carry

    lax.fori_loop(0, 4 * SLOT_TOTAL // 1024, backward, 0)
    out = jnp.concatenate([r.total[:, 0:512].T, r.total[:, 512:1024].T], 1)
    r.grad_z[...] = out.astype(BF).reshape(GROUP, COLUMNS, 128)


WIDE, NARROW, POINT_BLOCK = (GROUP, COLUMNS, 128), (GROUP, 16, 128), (GROUP, 128, 128)
INPUTS = (
    "x", "route", "live", "nbr", "cnt", "lists", "ew1", "ewo", "dw1", "dwo", "skip", "read",
    "weight", "sums", "pairs", "waves", "ky", "kx", "kxi", "kyi",
)
OUTPUTS = {
    "pred": ((1, SLOT_TOTAL), F32), "modes": ((64, 128), F32), "grads": ((64, 128), F32),
}
SCRATCH = {
    "send1": (POINT_BLOCK, BF), "recv1": (POINT_BLOCK, BF),
    "send2": (POINT_BLOCK, BF), "recv2": (POINT_BLOCK, BF),
    "regroup": ((GROUP, GROUP, CAPACITY, 128), F32), "slot": ((1, POINTS), jnp.int32),
    "tab": ((SLOT_TOTAL, 128), BF), "table": ((544, 256), BF), "pos_rows": ((32, 256), F32),
    "extra": ((8, 8, 256), F32), "target": ((8, 256), F32), "living": ((8, 256), F32),
    "high": ((COLUMNS // ENC_COLUMNS, 2048 * ENC_COLUMNS), jnp.int32),
    "prod": ((COLUMNS * 64, 2048), BF), "lat": ((COLUMNS * 64, DEPTH), BF),
    "z_rows": (WIDE, F32), "z": (WIDE, BF), "recv_a": (WIDE, BF), "send_b": (NARROW, BF),
    "recv_b": (NARROW, BF), "send_c": (NARROW, BF), "recv_c": (NARROW, BF),
    "send_d": (WIDE, BF), "recv_d": (WIDE, BF),
    "before": ((64, 4 * SLOT_TOTAL), F32), "kern": ((64, 4 * SLOT_TOTAL), F32),
    "basis": ((1024, 4 * SLOT_TOTAL), BF), "back_t": ((64, 1024), BF),
    "dots": ((8, 1024), F32), "total": ((64, 1024), F32),
    "grad_z": (WIDE, BF), "recv_e": (WIDE, BF), "send_f": (NARROW, BF), "recv_f": (NARROW, BF),
}
EXCHANGES = 8


def step_kernel(*refs):
    names = list(INPUTS) + list(OUTPUTS) + list(SCRATCH)
    for k in range(1, EXCHANGES + 1):
        names += [f"s{k}", f"r{k}"]
    r = types.SimpleNamespace(**dict(zip(names, refs)))
    send_points(r)
    encode(r)
    blocks = 4 * SLOT_TOTAL // PREP // 4
    fourier(r, lambda k: lambda: prepare(r, k * blocks, (k + 1) * blocks))
    decode(r)
    grads = forward_modes(
        r.grad_z, r, ((r.s7, r.r7), (r.s8, r.r8)), r.recv_e, r.send_f, r.recv_f,
        lambda k: None,
    )
    r.grads[...] = grads * own_doubling()


def step(*inputs):
    whole = pl.BlockSpec(memory_space=pltpu.VMEM)
    in_specs = [whole] * len(INPUTS)
    in_specs[INPUTS.index("live")] = pl.BlockSpec(memory_space=pltpu.SMEM)
    semaphores = [pltpu.SemaphoreType.DMA((GROUP,))] * (2 * EXCHANGES)
    return pl.pallas_call(
        step_kernel,
        out_shape=tuple(jax.ShapeDtypeStruct(*v) for v in OUTPUTS.values()),
        in_specs=in_specs,
        out_specs=(whole,) * len(OUTPUTS),
        scratch_shapes=[pltpu.VMEM(*v) for v in SCRATCH.values()] + semaphores,
        compiler_params=pltpu.CompilerParams(
            collective_id=0, has_side_effects=True, vmem_limit_bytes=VMEM_LIMIT
        ),
        name="training_step",
    )(*inputs)


def outer_kernel(modes_ref, grad_ref, out_ref):
    modes_t = modes_ref[...].T
    grads = grad_ref[...]
    swapped = pltpu.roll(grads, CHANNELS, 1) * lane_sign(grads.shape)
    for m in range(8):
        out_ref[m] = (
            modes_t[0:64, m : m + 1] * grads[m : m + 1]
            + modes_t[64:128, m : m + 1] * swapped[m : m + 1]
        )


def outer(modes, grads):
    return pl.pallas_call(
        outer_kernel,
        grid=(8,),
        out_shape=jax.ShapeDtypeStruct((64, 64, 128), F32),
        in_specs=[pl.BlockSpec((8, 128), lambda i: (i, 0))] * 2,
        out_specs=pl.BlockSpec((8, 64, 128), lambda i: (i, 0, 0)),
        compiler_params=pltpu.CompilerParams(vmem_limit_bytes=VMEM_LIMIT),
        name="outer",
    )(modes, grads)


def two_parts(values):
    high = lax.reduce_precision(values, 8, 7)
    return high.astype(BF), (values - high).astype(BF)


def encoder_first(weight, bias):
    high, low = two_parts(weight * 0.5)
    bias_high, bias_low = two_parts(bias * 0.5)
    return jnp.concatenate(
        [
            jnp.repeat(high, 8, axis=0), jnp.repeat(low, 8, axis=0),
            -high, -low, bias_high[None], bias_low[None],
        ],
        0,
    ).T


def decoder_first(weight, bias):
    high, low = two_parts(weight * 0.5)
    bias_high, bias_low = two_parts(bias * 0.5)
    return jnp.concatenate(
        [
            high, low, jnp.zeros((2, weight.shape[1]), BF),
            -high, -low, bias_high[None], bias_low[None],
        ],
        0,
    ).T


def body(
    point_features, positions, targets, routes, live_counts, cell_neighbours, cell_counts,
    slot_neighbours, encoder_in, encoder_bias, encoder_out, decoder_in, decoder_bias,
    decoder_out, skip_weight, spectral_weight, readout_weight,
):
    x = jnp.concatenate(
        [
            point_features, positions, targets[:, None],
            jnp.ones((POINTS, 1), BF), jnp.zeros((POINTS, 59), BF),
        ],
        1,
    )
    steps = COLUMNS // ENC_COLUMNS
    pred, modes, grads = step(
        x, routes.reshape(1, POINTS), live_counts,
        cell_neighbours.reshape(steps, -1), cell_counts.reshape(steps, -1), slot_neighbours,
        encoder_first(encoder_in, encoder_bias), encoder_out.T,
        decoder_first(decoder_in, decoder_bias), decoder_out.T, skip_weight.T,
        readout_weight[:, None], spectral_weight.reshape(64, 64, 128),
        jnp.asarray(entry_sums()), jnp.asarray(pair_sums()), jnp.asarray(depth_waves()),
        jnp.asarray(kron_forward_y()), jnp.asarray(kron_forward_x()),
        jnp.asarray(kron_inverse_x()), jnp.asarray(kron_inverse_y()),
    )
    return pred, outer(modes, grads).reshape(32, 2, 1, 64, 128)


def solution(mesh):
    in_specs = (
        P(("px", "py"), None), P(("px", "py"), None), P(("px", "py")), P(("px", "py"), None),
        P(("px", "py")), P("px", "py", None), P("px", "py", None), P(("px", "py"), None),
        P(), P(), P(), P(), P(), P(), P(),
        P(None, "px", "py", None, None), P(),
    )
    out_specs = (P(("px", "py"), None), P(None, "px", "py", None, None))
    return jax.shard_map(body, mesh=mesh, in_specs=in_specs, out_specs=out_specs, check_vma=False)
```

time: 229 us -> 144 us (0.63)
  Pallas kernels: 218 us -> 127 us
  local copies, waits for them, and re-layouts: 9.37 us -> 13 us
  other arithmetic: 0.04 us -> 2.74 us
    pallas_call x5 -> x1, Pallas kernels: 212 us -> 121 us  [step(): pl.pallas_call(step_kernel, out_shape=tuple((jax.ShapeDtypeStruct(*v) for...]
where the time goes in v2:
time: 144 us
  Pallas kernels  127 us (88%)
  local copies, waits for them, and re-layouts  13 us (9%)
  other arithmetic  2.74 us (2%)
    pallas_call x1, Pallas kernels, step(): pl.pallas_call(step_kernel, out_shape=tuple((jax.ShapeDtypeStruct(*v) for...  121 us
    pallas_call x1, Pallas kernels, outer(): pl.pallas_call(outer_kernel, grid=(8,), out_shape=jax.ShapeDtypeStruct((6...  5.52 us
    unnamed x6, local copies, waits for them, and re-layouts  3.97 us

profile of v2, /device:TPU:1, one launch (start us, length us, event | category | flops | bytes accessed | tf_op | source)
XLA Modules:
  0.0 143.6 jit_solution(1276514554003054971)
XLA Ops:
  1.3 0.7 fusion.5
  1.9 0.7 fusion.2
  2.6 0.7 broadcast_multiply_fusion
  3.3 0.7 fusion.6
  4.1 1.4 copy.87
  5.5 0.1 copy.85
  5.6 0.1 copy.84
  5.7 1.4 reshape.27.refs_4_
  7.1 1.3 copy.88.refs_11_
  8.4 0.1 copy.78
  8.5 0.1 copy.81
  8.6 0.1 copy.79
  8.7 0.1 copy.83
  8.8 0.1 copy.82
  9.0 0.7 concatenate.10
  9.7 0.7 copy.86
  10.4 1.1 copy.75
  11.5 0.9 copy.76
  12.4 0.9 broadcast_in_dim.44
  13.3 1.8 %reshape.26.refs_3_ = s32[16,4096]{1,0:T(8,128)} reshape(s32[8,4,2048]{2,1,0:T(4,128)} %param.29) | data formatting | bytes 524288 | tf_op jit(solution)/shard_map/reshape | solution.py:590
  15.2 1.3 concatenate.9.refs_0_
  16.4 121.0 %training_step.1 = (f32[1,2048]{1,0:T(1,128)}, f32[64,128]{1,0:T(8,128)}, f32[64,128]{1,0:T(8,128)}) custom-call(bf16[1024,128]{1,0:T(8,128)(2,1)} %concatenate.9.refs_0_, s32[1,1024]{1,0:T(1,128)} %bitcast.26, s32[1]{0:T(128)S(6)} %copy.91.refs_2_, s32[16,4096]{1,0:T(8,128)} %reshape.26.refs_3_, s32[16,512]{1,0:T(8,128)} %reshape.27.refs_4_, ...), custom_call_target="tpu_custom_call" | custom-call | tf_op jit(solution)/shard_map/training_step/pallas_call | solution.py:510
  137.5 0.0 copy-start
  137.5 5.5 %outer.1 = f32[64,64,128]{2,1,0:T(8,128)} custom-call(f32[64,128]{1,0:T(8,128)} %get-tuple-element.6.modes_ref, f32[64,128]{1,0:T(8,128)} %get-tuple-element.7.grad_ref), custom_call_target="tpu_custom_call" | custom-call | tf_op jit(solution)/shard_map/outer/pallas_call | solution.py:535
  143.0 0.0 copy-done
  143.0 0.6 copy.92
  (9 shorter events, 0.2 us)
Async XLA Ops:
  137.5 5.5 %copy-start = (f32[1,2048]{1,0:T(1,128)S(1)}, f32[1,2048]{1,0:T(1,128)}, u32[]{:S(2)}) copy-start(f32[1,2048]{1,0:T(1,128)} %get-tuple-element.34) | copy-start | bytes 24580

commit v3 on v2

--- a/solution.py
+++ b/solution.py
@@ -25,6 +25,7 @@
 VMEM_LIMIT = 60 * 1024 * 1024
 ENC_COLUMNS = 2
 PREP = 512
+OUTER = 16
 POST = 2048
 
 
@@ -85,14 +86,6 @@
 def depth_waves():
     cos, sin = wave(256, np.arange(16), np.arange(256))
     return bf16_of(np.concatenate([cos, -sin]))
-
-
-def entry_sums():
-    return bf16_of(np.arange(2048)[:, None] // 8 == np.arange(256)[None, :])
-
-
-def pair_sums():
-    return bf16_of(np.arange(1024)[:, None] // 4 == np.arange(256)[None, :])
 
 
 def nt(left, right):
@@ -189,7 +182,14 @@
     finish(axis, send, recv, *pair)
 
 
-def send_points(r):
+def pick_rows(rows, sub):
+    out = jnp.zeros(sub.shape, F32)
+    for k, row in enumerate(rows):
+        out = jnp.where(sub == k, row, out)
+    return out
+
+
+def send_points(r, meanwhile):
     greet()
     live = r.live[0]
     lanes = lax.broadcasted_iota(jnp.int32, (1, POINTS), 1)
@@ -203,16 +203,33 @@
         0.0,
     ).astype(BF)
     counted = mm(named.astype(BF), earlier)
-    rank = jnp.sum(named * counted, axis=0, keepdims=True)
-    r.slot[...] = jnp.where(target < 256, target * CAPACITY + rank.astype(jnp.int32), -1)
+    rank = jnp.sum(named * counted, axis=0, keepdims=True).astype(jnp.int32)
+    kept = target < 256
+    r.slot[...] = jnp.where(kept, target * CAPACITY + rank, -1)
+    features = r.features[...]
+    r.twice[...] = jnp.concatenate([features, features], 0)
+    sub = lax.broadcasted_iota(jnp.int32, (8, POINTS), 0)
+    places = r.positions[...].astype(F32)
+    rest = pick_rows(
+        [places[0:1], places[1:2], places[2:3], r.targets[...].astype(F32), 1.0], sub
+    )
+    rows = lax.broadcasted_iota(jnp.int32, (128, POINTS), 0)
+    spread = jnp.where((rows >> 3) == (target & 15), jnp.concatenate([rest] * 16, 0), 0.0)
+    mine = jnp.where(kept, (target >> 4) * CAPACITY + rank, -1)
+    hot = jnp.where(rows == mine, 1.0, 0.0).astype(BF)
+    r.rest[...] = nt(hot, spread.astype(BF)).reshape(GROUP, 8, 128)
     greeted()
     a = lax.axis_index("px")
+    low_lanes = lax.broadcasted_iota(jnp.int32, (64, 128), 1) < 64
+    nothing = jnp.zeros((8, 128), F32)
 
     def pack(d, carry):
         peer = (a + d) & 15
-        rows = lax.broadcasted_iota(jnp.int32, (128, POINTS), 0) + peer * 128
-        hot = jnp.where(rows == r.slot[...], 1.0, 0.0).astype(BF)
-        r.send1[peer] = mm(hot, r.x[...]).astype(BF)
+        at = lax.broadcasted_iota(jnp.int32, (128, POINTS), 0) + peer * 128
+        hot = jnp.where(at == r.slot[...], 1.0, 0.0).astype(BF)
+        packed = nt(hot, r.twice[...])
+        r.send1[peer, 0:64] = jnp.where(low_lanes, packed[0:64], packed[64:128]).astype(BF)
+        r.send1[peer, 64:80] = jnp.concatenate([r.rest[peer], nothing], 0).astype(BF)
 
         @pl.when(d > 0)
         def _():
@@ -221,18 +238,99 @@
         return carry
 
     lax.fori_loop(0, GROUP, pack, 0)
+    meanwhile(0)()
     finish("px", r.send1, r.recv1, r.s1, r.r1)
     for source in range(GROUP):
-        r.regroup[source] = r.recv1[source].astype(F32).reshape(GROUP, CAPACITY, 128)
-    for dest in range(GROUP):
-        r.send2[dest] = r.regroup[:, dest].reshape(128, 128).astype(BF)
-    exchange("py", r.send2, r.recv2, (r.s2, r.r2))
-    for source in range(GROUP):
-        r.regroup[source] = r.recv2[source].astype(F32).reshape(GROUP, CAPACITY, 128)
-    for source in range(GROUP):
-        r.tab[source * 128 : (source + 1) * 128, :] = (
-            r.regroup[:, source].reshape(128, 128).astype(BF)
+        r.regroup[source] = r.recv1[source, 0:64].astype(F32).reshape(8, CAPACITY, 128)
+        r.rest[source] = r.recv1[source, 64:80].astype(F32)[0:8]
+    eye = identity(128)
+    rest = nt(eye, r.rest[...].reshape(128, 128).astype(BF))
+    for c in range(8):
+        first = r.regroup[0:8, c].reshape(64, 128)
+        second = r.regroup[8:16, c].reshape(64, 128)
+        r.send2[c, 0:64] = jnp.where(
+            low_lanes, first, pltpu.roll(second, 64, 1)
+        ).astype(BF)
+        r.send2[c + 8, 0:64] = jnp.where(
+            low_lanes, pltpu.roll(first, 64, 1), second
+        ).astype(BF)
+    for c in range(GROUP):
+        r.send2[c, 64:80] = jnp.concatenate([rest[c * 8 : c * 8 + 8], nothing], 0).astype(BF)
+    exchange("py", r.send2, r.recv2, (r.s2, r.r2), meanwhile(1))
+
+
+def slot_tables(r):
+    eye = identity(128)
+    low_lanes = lax.broadcasted_iota(jnp.int32, (8, 128), 1) < 64
+    r.pos_rows[...] = jnp.zeros(r.pos_rows.shape, F32)
+    for h in range(8):
+        rows = jnp.concatenate([r.recv2[2 * h, 0:64], r.recv2[2 * h + 1, 0:64]], 0)
+        flipped = nt(eye, rows).astype(BF)
+        r.table[h * 64 : (h + 1) * 64, 0:128] = flipped[0:64]
+        r.table[h * 64 : (h + 1) * 64, 128:256] = flipped[64:128]
+        even = r.recv2[2 * h, 64:80].astype(F32)[0:8]
+        odd = r.recv2[2 * h + 1, 64:80].astype(F32)[0:8]
+        r.rest[2 * h] = even
+        r.rest[2 * h + 1] = odd
+        left = jnp.where(low_lanes, even, pltpu.roll(odd, 64, 1))
+        right = jnp.where(low_lanes, pltpu.roll(even, 64, 1), odd)
+        for d in range(3):
+            r.pos_rows[d * 8 + h : d * 8 + h + 1, 0:128] = left[d : d + 1]
+            r.pos_rows[d * 8 + h : d * 8 + h + 1, 128:256] = right[d : d + 1]
+    r.table[512:544, :] = r.pos_rows[...].astype(BF)
+    by_slot = nt(eye, r.rest[...].reshape(128, 128).astype(BF))
+    rows = lax.broadcasted_iota(jnp.int32, (128, 128), 0)
+    lanes = lax.broadcasted_iota(jnp.int32, (128, 128), 1)
+    same = (rows >> 3) == (lanes >> 3)
+    sub = lax.broadcasted_iota(jnp.int32, (8, 128), 0)
+    part = lax.broadcasted_iota(jnp.int32, (8, 128), 1) & 7
+    wanted = jnp.where(sub < 3, sub, sub - 3)
+    chooser = jnp.where(part == wanted, 1.0, 0.0).astype(BF)
+    for a in range(GROUP):
+        spread = jnp.concatenate([by_slot[a * 8 : a * 8 + 8]] * 16, 0)
+        extra = nt(chooser, jnp.where(same, spread, 0.0).astype(BF))
+        h, half = a // 2, (a % 2) * 128
+        r.extra[h, :, half : half + 128] = extra
+        r.target[h : h + 1, half : half + 128] = extra[6:7]
+        r.living[h : h + 1, half : half + 128] = extra[7:8]
+
+
+def group_sums(r):
+    for ref, shift in ((r.sums, 3), (r.pairs, 2)):
+        rows = lax.broadcasted_iota(jnp.int32, ref.shape, 0)
+        lanes = lax.broadcasted_iota(jnp.int32, ref.shape, 1)
+        ref[...] = jnp.where((rows >> shift) == lanes, 1.0, 0.0).astype(BF)
+
+
+def first_layers(r):
+    def halves(values):
+        high = (values * 0.5).astype(BF).astype(F32)
+        return high, values * 0.5 - high
+
+    high, low = halves(r.ein[...])
+    bias_high, bias_low = halves(r.ebias[...])
+    sub = lax.broadcasted_iota(jnp.int32, (8, 80), 0)
+    rows = [jnp.broadcast_to(part[d : d + 1], (8, 80)) for part in (high, low) for d in range(3)]
+    rows.append(
+        pick_rows(
+            [-part[d : d + 1] for part in (high, low) for d in range(3)] + [bias_high, bias_low],
+            sub,
         )
+    )
+    r.ew1[...] = nt(identity(80), jnp.concatenate(rows, 0).astype(BF)).astype(BF)
+    high, low = halves(r.din[...])
+    bias_high, bias_low = halves(r.dbias[...])
+    sub = lax.broadcasted_iota(jnp.int32, (8, 256), 0)
+    positive = [part[d : d + 1] for part in (high, low) for d in range(3)]
+    negative = [-row for row in positive] + [bias_high, bias_low]
+    rows = jnp.concatenate([pick_rows(positive, sub), pick_rows(negative, sub)], 0)
+    r.dw1[...] = nt(identity(256), rows.astype(BF)).astype(BF)
+    r.skip_t[...] = nt(identity(64), r.skip[...]).astype(BF)
+    rows = lax.broadcasted_iota(jnp.int32, (64, 64), 0)
+    lanes = lax.broadcasted_iota(jnp.int32, (64, 64), 1)
+    r.read[...] = jnp.sum(
+        jnp.where(rows == lanes, r.readout[...], 0.0), axis=1, keepdims=True
+    )
 
 
 def first_layer_centres(ij, depth, sub):
@@ -245,35 +343,26 @@
     )
 
 
+def place_lists(r):
+    for i in range(8):
+        r.counts[i * 4 : (i + 1) * 4, :] = r.cnt[i].astype(F32)
+        r.low[i * 4 : (i + 1) * 4, :] = r.nbr[i]
+    spread = nt(r.counts[...].astype(BF), r.sums[...])
+    places = (lax.broadcasted_iota(jnp.int32, (COLUMNS, 2048), 1) & 7).astype(F32)
+    ids = r.low[...]
+    r.high[...] = jnp.where(places < spread, (ids >> 4) & 7, 8)
+    r.low[...] = (
+        ((ids >> 10) << 7) + (((ids >> 3) & 1) << 6) + (((ids >> 7) & 7) << 3) + (ids & 7)
+    )
+
+
 def encode(r):
-    eye = identity(128)
-    picks = lax.broadcasted_iota(jnp.int32, (8, 128), 0)
-    lanes8 = lax.broadcasted_iota(jnp.int32, (8, 128), 1)
-    wanted = jnp.where(picks < 3, picks + 64, picks + 61)
-    chooser = jnp.where(lanes8 == wanted, 1.0, 0.0).astype(BF)
-    r.pos_rows[...] = jnp.zeros(r.pos_rows.shape, F32)
-    for h in range(8):
-        rows = r.tab[h * 256 : (h + 1) * 256, :]
-        r.table[h * 64 : (h + 1) * 64, :] = nt(eye, rows)[0:64].astype(BF)
-        extra = nt(chooser, rows)
-        r.extra[h] = extra
-        r.target[h : h + 1, :] = extra[6:7]
-        r.living[h : h + 1, :] = extra[7:8]
-        for d in range(3):
-            r.pos_rows[d * 8 + h : d * 8 + h + 1, :] = extra[d : d + 1]
-    r.table[512:544, :] = r.pos_rows[...].astype(BF)
-    counts = r.cnt[...].astype(F32)
-    steps = COLUMNS // ENC_COLUMNS
-    places = (lax.broadcasted_iota(jnp.int32, (steps, 2048), 1) & 7).astype(F32)
-    for k in range(ENC_COLUMNS):
-        spread = nt(counts[:, k * DEPTH : (k + 1) * DEPTH].astype(BF), r.sums[...])
-        ids = r.nbr[:, k * 2048 : (k + 1) * 2048]
-        r.high[:, k * 2048 : (k + 1) * 2048] = jnp.where(places < spread, ids >> 8, 8)
     n = 2048 * ENC_COLUMNS
 
     def columns(step, carry):
-        low = r.nbr[pl.ds(step, 1), :] & 255
-        high = r.high[pl.ds(step, 1), :]
+        rows = [step * ENC_COLUMNS + k for k in range(ENC_COLUMNS)]
+        low = jnp.concatenate([r.low[pl.ds(row, 1), :] for row in rows], 1)
+        high = jnp.concatenate([r.high[pl.ds(row, 1), :] for row in rows], 1)
         hot = jnp.where(
             lax.broadcasted_iota(jnp.int32, (256, n), 0) == low, 1.0, 0.0
         ).astype(BF)
@@ -299,17 +388,15 @@
             r.prod[pl.ds(row, 64), :] = shares[:, k * 2048 : (k + 1) * 2048]
         return carry
 
-    lax.fori_loop(0, steps, columns, 0)
-    shares = 1.0 / counts
+    lax.fori_loop(0, COLUMNS // ENC_COLUMNS, columns, 0)
+    shares = 1.0 / r.counts[...]
     group = 8
     for g in range(COLUMNS // group):
         latent = mm(r.prod[g * group * 64 : (g + 1) * group * 64, :], r.sums[...])
         for k in range(group):
             ij = g * group + k
-            row, part = ij // ENC_COLUMNS, ij % ENC_COLUMNS
-            share = shares[row : row + 1, part * DEPTH : (part + 1) * DEPTH]
             r.lat[ij * 64 : (ij + 1) * 64, :] = (
-                latent[k * 64 : (k + 1) * 64] * share
+                latent[k * 64 : (k + 1) * 64] * shares[ij : ij + 1]
             ).astype(BF)
     both = nt(r.waves[...], r.lat[...])
     for ij in range(COLUMNS):
@@ -368,6 +455,25 @@
     exchange("py", r.send_d, r.recv_d, (r.s6, r.r6), meanwhile(3))
 
 
+def depth_basis(r):
+    n = PREP
+
+    def block(step, carry):
+        here = pl.ds(pl.multiple_of(step * n, n), n)
+        cells = r.lists[:, here]
+        low, column = cells & 255, cells >> 8
+        hot = jnp.where(
+            lax.broadcasted_iota(jnp.int32, (256, n), 0) == low, 1.0, 0.0
+        ).astype(BF)
+        tw = mm(r.waves[...], hot)
+        match = lax.broadcasted_iota(jnp.int32, (COLUMNS, n), 0) == column
+        for q in range(32):
+            r.basis[q * 32 : (q + 1) * 32, here] = jnp.where(match, tw[q : q + 1], 0.0).astype(BF)
+        return carry
+
+    lax.fori_loop(0, 4 * SLOT_TOTAL // n, block, 0)
+
+
 def prepare(r, first, last):
     n = PREP
 
@@ -389,13 +495,7 @@
         for k in range(COLUMNS):
             part = found[k * 64 : (k + 1) * 64].reshape(8, 8, n)
             near = jnp.where((column8 == k)[None], part, near)
-        r.before[:, pl.ds(off, n)] = mm(r.skip[...], near.reshape(64, n).astype(BF))
-        tw = mm(r.waves[...], hot)
-        match = lax.broadcasted_iota(jnp.int32, (COLUMNS, n), 0) == column
-        for q in range(32):
-            r.basis[q * 32 : (q + 1) * 32, pl.ds(off, n)] = jnp.where(
-                match, tw[q : q + 1], 0.0
-            ).astype(BF)
+        r.before[:, pl.ds(off, n)] = mm(r.skip_t[...], near.reshape(64, n).astype(BF))
         sub = lax.broadcasted_iota(jnp.int32, (8, n), 0)
         stacked = jnp.concatenate(
             [expanded, first_layer_centres(column, low, sub)], 0
@@ -458,10 +558,11 @@
     r.grad_z[...] = out.astype(BF).reshape(GROUP, COLUMNS, 128)
 
 
-WIDE, NARROW, POINT_BLOCK = (GROUP, COLUMNS, 128), (GROUP, 16, 128), (GROUP, 128, 128)
+WIDE, NARROW, POINT_BLOCK = (GROUP, COLUMNS, 128), (GROUP, 16, 128), (GROUP, 80, 128)
 INPUTS = (
-    "x", "route", "live", "nbr", "cnt", "lists", "ew1", "ewo", "dw1", "dwo", "skip", "read",
-    "weight", "sums", "pairs", "waves", "ky", "kx", "kxi", "kyi",
+    "features", "positions", "targets", "route", "live", "nbr", "cnt", "lists",
+    "ein", "ebias", "ewo", "din", "dbias", "dwo", "skip", "readout",
+    "weight", "waves", "ky", "kx", "kxi", "kyi",
 )
 OUTPUTS = {
     "pred": ((1, SLOT_TOTAL), F32), "modes": ((64, 128), F32), "grads": ((64, 128), F32),
@@ -469,10 +570,13 @@
 SCRATCH = {
     "send1": (POINT_BLOCK, BF), "recv1": (POINT_BLOCK, BF),
     "send2": (POINT_BLOCK, BF), "recv2": (POINT_BLOCK, BF),
-    "regroup": ((GROUP, GROUP, CAPACITY, 128), F32), "slot": ((1, POINTS), jnp.int32),
-    "tab": ((SLOT_TOTAL, 128), BF), "table": ((544, 256), BF), "pos_rows": ((32, 256), F32),
+    "regroup": ((GROUP, 8, CAPACITY, 128), F32), "rest": ((GROUP, 8, 128), F32),
+    "slot": ((1, POINTS), jnp.int32), "twice": ((128, POINTS), BF),
+    "sums": ((2048, 256), BF), "pairs": ((1024, 256), BF), "ew1": ((80, 56), BF), "dw1": ((256, 16), BF), "skip_t": ((64, 64), BF),
+    "read": ((64, 1), F32), "counts": ((COLUMNS, DEPTH), F32), "low": ((COLUMNS, 2048), jnp.int32),
+    "table": ((544, 256), BF), "pos_rows": ((32, 256), F32),
     "extra": ((8, 8, 256), F32), "target": ((8, 256), F32), "living": ((8, 256), F32),
-    "high": ((COLUMNS // ENC_COLUMNS, 2048 * ENC_COLUMNS), jnp.int32),
+    "high": ((COLUMNS, 2048), jnp.int32),
     "prod": ((COLUMNS * 64, 2048), BF), "lat": ((COLUMNS * 64, DEPTH), BF),
     "z_rows": (WIDE, F32), "z": (WIDE, BF), "recv_a": (WIDE, BF), "send_b": (NARROW, BF),
     "recv_b": (NARROW, BF), "send_c": (NARROW, BF), "recv_c": (NARROW, BF),
@@ -490,7 +594,14 @@
     for k in range(1, EXCHANGES + 1):
         names += [f"s{k}", f"r{k}"]
     r = types.SimpleNamespace(**dict(zip(names, refs)))
-    send_points(r)
+
+    def before_points():
+        group_sums(r)
+        first_layers(r)
+        place_lists(r)
+
+    send_points(r, lambda k: before_points if k == 0 else lambda: depth_basis(r))
+    slot_tables(r)
     encode(r)
     blocks = 4 * SLOT_TOTAL // PREP // 4
     fourier(r, lambda k: lambda: prepare(r, k * blocks, (k + 1) * blocks))
@@ -524,7 +635,7 @@
     modes_t = modes_ref[...].T
     grads = grad_ref[...]
     swapped = pltpu.roll(grads, CHANNELS, 1) * lane_sign(grads.shape)
-    for m in range(8):
+    for m in range(OUTER):
         out_ref[m] = (
             modes_t[0:64, m : m + 1] * grads[m : m + 1]
             + modes_t[64:128, m : m + 1] * swapped[m : m + 1]
@@ -534,42 +645,13 @@
 def outer(modes, grads):
     return pl.pallas_call(
         outer_kernel,
-        grid=(8,),
+        grid=(64 // OUTER,),
         out_shape=jax.ShapeDtypeStruct((64, 64, 128), F32),
-        in_specs=[pl.BlockSpec((8, 128), lambda i: (i, 0))] * 2,
-        out_specs=pl.BlockSpec((8, 64, 128), lambda i: (i, 0, 0)),
+        in_specs=[pl.BlockSpec((OUTER, 128), lambda i: (i, 0))] * 2,
+        out_specs=pl.BlockSpec((OUTER, 64, 128), lambda i: (i, 0, 0)),
         compiler_params=pltpu.CompilerParams(vmem_limit_bytes=VMEM_LIMIT),
         name="outer",
     )(modes, grads)
-
-
-def two_parts(values):
-    high = lax.reduce_precision(values, 8, 7)
-    return high.astype(BF), (values - high).astype(BF)
-
-
-def encoder_first(weight, bias):
-    high, low = two_parts(weight * 0.5)
-    bias_high, bias_low = two_parts(bias * 0.5)
-    return jnp.concatenate(
-        [
-            jnp.repeat(high, 8, axis=0), jnp.repeat(low, 8, axis=0),
-            -high, -low, bias_high[None], bias_low[None],
-        ],
-        0,
-    ).T
-
-
-def decoder_first(weight, bias):
-    high, low = two_parts(weight * 0.5)
-    bias_high, bias_low = two_parts(bias * 0.5)
-    return jnp.concatenate(
-        [
-            high, low, jnp.zeros((2, weight.shape[1]), BF),
-            -high, -low, bias_high[None], bias_low[None],
-        ],
-        0,
-    ).T
 
 
 def body(
@@ -577,21 +659,13 @@
     slot_neighbours, encoder_in, encoder_bias, encoder_out, decoder_in, decoder_bias,
     decoder_out, skip_weight, spectral_weight, readout_weight,
 ):
-    x = jnp.concatenate(
-        [
-            point_features, positions, targets[:, None],
-            jnp.ones((POINTS, 1), BF), jnp.zeros((POINTS, 59), BF),
-        ],
-        1,
-    )
-    steps = COLUMNS // ENC_COLUMNS
     pred, modes, grads = step(
-        x, routes.reshape(1, POINTS), live_counts,
-        cell_neighbours.reshape(steps, -1), cell_counts.reshape(steps, -1), slot_neighbours,
-        encoder_first(encoder_in, encoder_bias), encoder_out.T,
-        decoder_first(decoder_in, decoder_bias), decoder_out.T, skip_weight.T,
-        readout_weight[:, None], spectral_weight.reshape(64, 64, 128),
-        jnp.asarray(entry_sums()), jnp.asarray(pair_sums()), jnp.asarray(depth_waves()),
+        point_features.T, positions.T, targets[None], routes.reshape(1, POINTS), live_counts,
+        cell_neighbours, cell_counts, slot_neighbours,
+        encoder_in, encoder_bias[None], encoder_out.T,
+        decoder_in, decoder_bias[None], decoder_out.T, skip_weight, readout_weight[None],
+        spectral_weight.reshape(64, 64, 128),
+        jnp.asarray(depth_waves()),
         jnp.asarray(kron_forward_y()), jnp.asarray(kron_forward_x()),
         jnp.asarray(kron_inverse_x()), jnp.asarray(kron_inverse_y()),
     )

time: 144 us -> 120 us (0.83)
  local copies, waits for them, and re-layouts: 13 us -> 1.88 us
  Pallas kernels: 127 us -> 117 us
  other arithmetic: 2.74 us -> 0 us
    pallas_call x1, Pallas kernels: 121 us -> 113 us  [step(): pl.pallas_call(step_kernel, out_shape=tuple((jax.ShapeDtypeStruct(*v) for...]
    reshape x6 -> x0, local copies, waits for them, and re-layouts: 3.41 us -> none  [the longest x1 1.81 us: body(): cell_neighbours.reshape(steps, -1)]
    unnamed x6 -> x3, local copies, waits for them, and re-layouts: 3.97 us -> 0.6 us
    concatenate x4 -> x0, local copies, waits for them, and re-layouts: 2.77 us -> none  [the longest x1 1.26 us: body(): jnp.concatenate([point_features, positions, targets[:, None], jnp.ones((P...]
    pallas_call x1, Pallas kernels: 5.52 us -> 3.96 us  [outer(): pl.pallas_call(outer_kernel, grid=(64 // OUTER,), out_shape=jax.ShapeDtyp...]
where the time goes in v3:
time: 120 us
  Pallas kernels  117 us (98%)
  local copies, waits for them, and re-layouts  1.88 us (2%)
  between operations  1.29 us (1%)
    pallas_call x1, Pallas kernels, step(): pl.pallas_call(step_kernel, out_shape=tuple((jax.ShapeDtypeStruct(*v) for...  113 us
    pallas_call x1, Pallas kernels, outer(): pl.pallas_call(outer_kernel, grid=(64 // OUTER,), out_shape=jax.ShapeDtyp...  3.96 us

profile of v3, /device:TPU:1, one launch (start us, length us, event | category | flops | bytes accessed | tf_op | source)
XLA Modules:
  0.0 119.8 jit_solution(13753071407687793042)
XLA Ops:
  1.3 1.3 %broadcast_in_dim.12.refs_2_ = bf16[1,1024]{1,0:T(2,128)(2,1)} reshape(bf16[1024]{0:T(1024)(128)(2,1)} %param.24) | data formatting | bytes 4096 | tf_op jit(solution)/shard_map/broadcast_in_dim | solution.py:663
  2.6 112.7 %training_step.1 = (f32[1,2048]{1,0:T(1,128)}, f32[64,128]{1,0:T(8,128)}, f32[64,128]{1,0:T(8,128)}) custom-call(bf16[64,1024]{1,0:T(8,128)(2,1)} %bitcast.14, bf16[3,1024]{1,0:T(4,128)(2,1)} %bitcast.17, bf16[1,1024]{1,0:T(2,128)(2,1)} %broadcast_in_dim.12.refs_2_, s32[1,1024]{1,0:T(1,128)} %bitcast.18, s32[1]{0:T(128)S(6)} %copy.26.refs_4_, ...), custom_call_target="tpu_custom_call" | custom-call | tf_op jit(solution)/shard_map/training_step/pallas_call | solution.py:621
  115.3 0.0 copy-start
  115.3 4.0 %outer.1 = f32[64,64,128]{2,1,0:T(8,128)} custom-call(f32[64,128]{1,0:T(8,128)} %get-tuple-element.6.modes_ref, f32[64,128]{1,0:T(8,128)} %get-tuple-element.7.grad_ref), custom_call_target="tpu_custom_call" | custom-call | tf_op jit(solution)/shard_map/outer/pallas_call | solution.py:646
  119.2 0.0 copy-done
  119.2 0.6 copy.27
Async XLA Ops:
  115.3 4.0 %copy-start = (f32[1,2048]{1,0:T(1,128)S(1)}, f32[1,2048]{1,0:T(1,128)}, u32[]{:S(2)}) copy-start(f32[1,2048]{1,0:T(1,128)} %get-tuple-element.12) | copy-start | bytes 24580

commit v4 on v3

--- a/solution.py
+++ b/solution.py
@@ -25,7 +25,7 @@
 VMEM_LIMIT = 60 * 1024 * 1024
 ENC_COLUMNS = 2
 PREP = 512
-OUTER = 16
+OUTER = 32
 POST = 2048
 
 
@@ -210,9 +210,9 @@
     r.twice[...] = jnp.concatenate([features, features], 0)
     sub = lax.broadcasted_iota(jnp.int32, (8, POINTS), 0)
     places = r.positions[...].astype(F32)
-    rest = pick_rows(
-        [places[0:1], places[1:2], places[2:3], r.targets[...].astype(F32), 1.0], sub
-    )
+    wanted = r.targets[...].astype(F32)
+    wanted = jnp.concatenate([wanted[k : k + 1] for k in range(8)], 1)
+    rest = pick_rows([places[0:1], places[1:2], places[2:3], wanted, 1.0], sub)
     rows = lax.broadcasted_iota(jnp.int32, (128, POINTS), 0)
     spread = jnp.where((rows >> 3) == (target & 15), jnp.concatenate([rest] * 16, 0), 0.0)
     mine = jnp.where(kept, (target >> 4) * CAPACITY + rank, -1)
@@ -223,21 +223,24 @@
     low_lanes = lax.broadcasted_iota(jnp.int32, (64, 128), 1) < 64
     nothing = jnp.zeros((8, 128), F32)
 
-    def pack(d, carry):
-        peer = (a + d) & 15
-        at = lax.broadcasted_iota(jnp.int32, (128, POINTS), 0) + peer * 128
+    def pack(step, carry):
+        group = ((a >> 2) + 2 + step) & 3
+        at = lax.broadcasted_iota(jnp.int32, (512, POINTS), 0) + group * 512
         hot = jnp.where(at == r.slot[...], 1.0, 0.0).astype(BF)
         packed = nt(hot, r.twice[...])
-        r.send1[peer, 0:64] = jnp.where(low_lanes, packed[0:64], packed[64:128]).astype(BF)
-        r.send1[peer, 64:80] = jnp.concatenate([r.rest[peer], nothing], 0).astype(BF)
-
-        @pl.when(d > 0)
-        def _():
-            copy_to("px", d, r.send1, r.recv1, r.s1, r.r1).start()
+        for k in range(4):
+            peer = group * 4 + k
+            block = packed[k * 128 : (k + 1) * 128]
+            r.send1[peer, 0:64] = jnp.where(low_lanes, block[0:64], block[64:128]).astype(BF)
+            r.send1[peer, 64:80] = jnp.concatenate([r.rest[peer], nothing], 0).astype(BF)
+
+            @pl.when(peer != a)
+            def _():
+                copy_to("px", (peer - a) & 15, r.send1, r.recv1, r.s1, r.r1).start()
 
         return carry
 
-    lax.fori_loop(0, GROUP, pack, 0)
+    lax.fori_loop(0, 4, pack, 0)
     meanwhile(0)()
     finish("px", r.send1, r.recv1, r.s1, r.r1)
     for source in range(GROUP):
@@ -295,6 +298,13 @@
         r.living[h : h + 1, half : half + 128] = extra[7:8]
 
 
+def fetches(r):
+    return [
+        pltpu.make_async_copy(getattr(r, name + "_far"), getattr(r, name), r.fetched.at[k])
+        for k, name in enumerate(FETCHED)
+    ]
+
+
 def group_sums(r):
     for ref, shift in ((r.sums, 3), (r.pairs, 2)):
         rows = lax.broadcasted_iota(jnp.int32, ref.shape, 0)
@@ -545,16 +555,14 @@
     residue = living * (pred - r.target[...]) * 0.25
     spread = nt(parts_of(residue, 2), r.pairs[...])
     r.dots[...] = spread[0:8] + spread[8:16]
-    r.total[...] = jnp.zeros(r.total.shape, F32)
-
-    def backward(step, carry):
-        here = pl.ds(pl.multiple_of(step * 1024, 1024), 1024)
-        shares = (r.kern[:, here] * r.dots[pl.ds(step, 1), :]).astype(BF)
-        r.total[...] += nt(shares, r.basis[:, here])
-        return carry
-
-    lax.fori_loop(0, 4 * SLOT_TOTAL // 1024, backward, 0)
-    out = jnp.concatenate([r.total[:, 0:512].T, r.total[:, 512:1024].T], 1)
+    n = 4 * 1024
+    for step in range(4 * SLOT_TOTAL // n):
+        here = slice(step * n, (step + 1) * n)
+        rows = [r.dots[k : k + 1] for k in range(step * (n // 1024), (step + 1) * (n // 1024))]
+        shares = (r.kern[:, here] * jnp.concatenate(rows, 1)).astype(BF)
+        part = nt(r.basis[:, here], shares)
+        r.total[...] = part if step == 0 else r.total[...] + part
+    out = jnp.concatenate([r.total[0:512], r.total[512:1024]], 1)
     r.grad_z[...] = out.astype(BF).reshape(GROUP, COLUMNS, 128)
 
 
@@ -562,8 +570,12 @@
 INPUTS = (
     "features", "positions", "targets", "route", "live", "nbr", "cnt", "lists",
     "ein", "ebias", "ewo", "din", "dbias", "dwo", "skip", "readout",
-    "weight", "waves", "ky", "kx", "kxi", "kyi",
+    "waves", "weight_far", "ky_far", "kx_far", "kxi_far", "kyi_far",
 )
+FETCHED = {
+    "weight": (64, 64, 128), "ky": (512, 512), "kx": (128, 256), "kxi": (512, 64),
+    "kyi": (1024, 256),
+}
 OUTPUTS = {
     "pred": ((1, SLOT_TOTAL), F32), "modes": ((64, 128), F32), "grads": ((64, 128), F32),
 }
@@ -583,8 +595,9 @@
     "send_d": (WIDE, BF), "recv_d": (WIDE, BF),
     "before": ((64, 4 * SLOT_TOTAL), F32), "kern": ((64, 4 * SLOT_TOTAL), F32),
     "basis": ((1024, 4 * SLOT_TOTAL), BF), "back_t": ((64, 1024), BF),
-    "dots": ((8, 1024), F32), "total": ((64, 1024), F32),
+    "dots": ((8, 1024), F32), "total": ((1024, 64), F32),
     "grad_z": (WIDE, BF), "recv_e": (WIDE, BF), "send_f": (NARROW, BF), "recv_f": (NARROW, BF),
+    **{name: (shape, BF) for name, shape in FETCHED.items()},
 }
 EXCHANGES = 8
 
@@ -593,6 +606,7 @@
     names = list(INPUTS) + list(OUTPUTS) + list(SCRATCH)
     for k in range(1, EXCHANGES + 1):
         names += [f"s{k}", f"r{k}"]
+    names.append("fetched")
     r = types.SimpleNamespace(**dict(zip(names, refs)))
 
     def before_points():
@@ -600,9 +614,13 @@
         first_layers(r)
         place_lists(r)
 
+    for fetch in fetches(r):
+        fetch.start()
     send_points(r, lambda k: before_points if k == 0 else lambda: depth_basis(r))
     slot_tables(r)
     encode(r)
+    for fetch in fetches(r):
+        fetch.wait()
     blocks = 4 * SLOT_TOTAL // PREP // 4
     fourier(r, lambda k: lambda: prepare(r, k * blocks, (k + 1) * blocks))
     decode(r)
@@ -617,7 +635,10 @@
     whole = pl.BlockSpec(memory_space=pltpu.VMEM)
     in_specs = [whole] * len(INPUTS)
     in_specs[INPUTS.index("live")] = pl.BlockSpec(memory_space=pltpu.SMEM)
+    for name in FETCHED:
+        in_specs[INPUTS.index(name + "_far")] = pl.BlockSpec(memory_space=pl.ANY)
     semaphores = [pltpu.SemaphoreType.DMA((GROUP,))] * (2 * EXCHANGES)
+    semaphores.append(pltpu.SemaphoreType.DMA((len(FETCHED),)))
     return pl.pallas_call(
         step_kernel,
         out_shape=tuple(jax.ShapeDtypeStruct(*v) for v in OUTPUTS.values()),
@@ -660,12 +681,11 @@
     decoder_out, skip_weight, spectral_weight, readout_weight,
 ):
     pred, modes, grads = step(
-        point_features.T, positions.T, targets[None], routes.reshape(1, POINTS), live_counts,
+        point_features.T, positions.T, targets.reshape(8, 128), routes.reshape(1, POINTS), live_counts,
         cell_neighbours, cell_counts, slot_neighbours,
         encoder_in, encoder_bias[None], encoder_out.T,
         decoder_in, decoder_bias[None], decoder_out.T, skip_weight, readout_weight[None],
-        spectral_weight.reshape(64, 64, 128),
-        jnp.asarray(depth_waves()),
+        jnp.asarray(depth_waves()), spectral_weight.reshape(64, 64, 128),
         jnp.asarray(kron_forward_y()), jnp.asarray(kron_forward_x()),
         jnp.asarray(kron_inverse_x()), jnp.asarray(kron_inverse_y()),
     )

time: 120 us -> 114 us (0.950)
  Pallas kernels: 117 us -> 112 us
  local copies, waits for them, and re-layouts: 1.88 us -> 0.6 us
    pallas_call x1, Pallas kernels: 113 us -> 109 us  [step(): pl.pallas_call(step_kernel, out_shape=tuple((jax.ShapeDtypeStruct(*v) for...]
    broadcast_in_dim x1 -> x0, local copies, waits for them, and re-layouts: 1.28 us -> none  [body(): targets[None]]
where the time goes in v4:
time: 114 us
  Pallas kernels  112 us (98%)
  between operations  1.3 us (1%)
    pallas_call x1, Pallas kernels, step(): pl.pallas_call(step_kernel, out_shape=tuple((jax.ShapeDtypeStruct(*v) for...  109 us
    pallas_call x1, Pallas kernels, outer(): pl.pallas_call(outer_kernel, grid=(64 // OUTER,), out_shape=jax.ShapeDtyp...  3.26 us

profile of v4, /device:TPU:1, one launch (start us, length us, event | category | flops | bytes accessed | tf_op | source)
XLA Modules:
  0.0 114.3 jit_solution(2243046532893010390)
XLA Ops:
  1.3 109.2 %training_step.1 = (f32[1,2048]{1,0:T(1,128)}, f32[64,128]{1,0:T(8,128)}, f32[64,128]{1,0:T(8,128)}) custom-call(bf16[64,1024]{1,0:T(8,128)(2,1)} %bitcast.15, bf16[3,1024]{1,0:T(4,128)(2,1)} %bitcast.18, bf16[8,128]{1,0:T(8,128)(2,1)} %bitcast.20, s32[1,1024]{1,0:T(1,128)} %bitcast.19, s32[1]{0:T(128)S(6)} %copy.26.refs_4_, s32[8,4,2048]{2,1,0:T(4,128)} %refs_5_.1, ...), custom_call_target="tpu_custom_call" | custom-call | tf_op jit(solution)/shard_map/training_step/pallas_call | solution.py:642
  110.4 0.0 copy-start
  110.5 3.3 %outer.1 = f32[64,64,128]{2,1,0:T(8,128)} custom-call(f32[64,128]{1,0:T(8,128)} %get-tuple-element.6.modes_ref, f32[64,128]{1,0:T(8,128)} %get-tuple-element.7.grad_ref), custom_call_target="tpu_custom_call" | custom-call | tf_op jit(solution)/shard_map/outer/pallas_call | solution.py:667
  113.7 0.0 copy-done
  113.7 0.6 copy.27
Async XLA Ops:
  110.4 3.3 %copy-start = (f32[1,2048]{1,0:T(1,128)S(1)}, f32[1,2048]{1,0:T(1,128)}, u32[]{:S(2)}) copy-start(f32[1,2048]{1,0:T(1,128)} %get-tuple-element.12) | copy-start | bytes 24580

commit v5 on v4

--- a/solution.py
+++ b/solution.py
@@ -25,7 +25,7 @@
 VMEM_LIMIT = 60 * 1024 * 1024
 ENC_COLUMNS = 2
 PREP = 512
-OUTER = 32
+OUTER = 16
 POST = 2048
 
 
@@ -398,7 +398,7 @@
             r.prod[pl.ds(row, 64), :] = shares[:, k * 2048 : (k + 1) * 2048]
         return carry
 
-    lax.fori_loop(0, COLUMNS // ENC_COLUMNS, columns, 0)
+    lax.fori_loop(0, COLUMNS // ENC_COLUMNS, columns, 0, unroll=2)
     shares = 1.0 / r.counts[...]
     group = 8
     for g in range(COLUMNS // group):
@@ -418,7 +418,8 @@
 
 
 def forward_modes(z, r, pairs, recv_a, send_b, recv_b, meanwhile):
-    exchange("py", z, recv_a, pairs[0], meanwhile(0))
+    meanwhile(0)()
+    finish("py", z, recv_a, *pairs[0])
     u = mm(r.ky[...], recv_a[...].reshape(512, 128))
     send_b[...] = turned(u[:256], u[256:], 1.0).astype(BF).reshape(GROUP, 16, 128)
     exchange("px", send_b, recv_b, pairs[1], meanwhile(1))
@@ -452,6 +453,7 @@
 
 
 def fourier(r, meanwhile):
+    start_all("py", r.z, r.recv_a, r.s3, r.r3)
     modes = forward_modes(
         r.z, r, ((r.s3, r.r3), (r.s4, r.r4)), r.recv_a, r.send_b, r.recv_b, meanwhile
     )
@@ -555,15 +557,39 @@
     residue = living * (pred - r.target[...]) * 0.25
     spread = nt(parts_of(residue, 2), r.pairs[...])
     r.dots[...] = spread[0:8] + spread[8:16]
+    for h in range(8):
+        here = slice(h * 1024, (h + 1) * 1024)
+        r.shares[:, here] = (r.kern[:, here] * r.dots[h : h + 1]).astype(BF)
+
+
+def gradient_depth_modes(r):
+    me = lax.axis_index("py")
     n = 4 * 1024
-    for step in range(4 * SLOT_TOTAL // n):
-        here = slice(step * n, (step + 1) * n)
-        rows = [r.dots[k : k + 1] for k in range(step * (n // 1024), (step + 1) * (n // 1024))]
-        shares = (r.kern[:, here] * jnp.concatenate(rows, 1)).astype(BF)
-        part = nt(r.basis[:, here], shares)
-        r.total[...] = part if step == 0 else r.total[...] + part
-    out = jnp.concatenate([r.total[0:512], r.total[512:1024]], 1)
-    r.grad_z[...] = out.astype(BF).reshape(GROUP, COLUMNS, 128)
+
+    def half(first):
+        depths = [(me + first + k) & 15 for k in range(8)]
+        starts = [pl.multiple_of(part * 512 + q * 32, 32) for part in range(2) for q in depths]
+        for step in range(4 * SLOT_TOTAL // n):
+            here = slice(step * n, (step + 1) * n)
+            waves = jnp.concatenate([r.basis[pl.ds(start, 32), here] for start in starts], 0)
+            part = nt(waves, r.shares[:, here])
+            r.total[...] = part if step == 0 else r.total[...] + part
+        for k, q in enumerate(depths):
+            real, imag = (r.total[256 * p + k * 32 : 256 * p + k * 32 + 32] for p in range(2))
+            r.grad_z[q] = jnp.concatenate([real, imag], 1).astype(BF)
+
+    def send(first, last):
+        def start(d, carry):
+            copy_to("py", d, r.grad_z, r.recv_e, r.s7, r.r7).start()
+            return carry
+
+        lax.fori_loop(first, last, start, 0)
+
+    half(4)
+    send(4, 12)
+    half(12)
+    send(12, 16)
+    send(1, 4)
 
 
 WIDE, NARROW, POINT_BLOCK = (GROUP, COLUMNS, 128), (GROUP, 16, 128), (GROUP, 80, 128)
@@ -595,7 +621,7 @@
     "send_d": (WIDE, BF), "recv_d": (WIDE, BF),
     "before": ((64, 4 * SLOT_TOTAL), F32), "kern": ((64, 4 * SLOT_TOTAL), F32),
     "basis": ((1024, 4 * SLOT_TOTAL), BF), "back_t": ((64, 1024), BF),
-    "dots": ((8, 1024), F32), "total": ((1024, 64), F32),
+    "dots": ((8, 1024), F32), "total": ((512, 64), F32), "shares": ((64, 4 * SLOT_TOTAL), BF),
     "grad_z": (WIDE, BF), "recv_e": (WIDE, BF), "send_f": (NARROW, BF), "recv_f": (NARROW, BF),
     **{name: (shape, BF) for name, shape in FETCHED.items()},
 }
@@ -624,9 +650,10 @@
     blocks = 4 * SLOT_TOTAL // PREP // 4
     fourier(r, lambda k: lambda: prepare(r, k * blocks, (k + 1) * blocks))
     decode(r)
+    gradient_depth_modes(r)
     grads = forward_modes(
         r.grad_z, r, ((r.s7, r.r7), (r.s8, r.r8)), r.recv_e, r.send_f, r.recv_f,
-        lambda k: None,
+        lambda k: lambda: None,
     )
     r.grads[...] = grads * own_doubling()
 
@@ -652,27 +679,41 @@
     )(*inputs)
 
 
-def outer_kernel(modes_ref, grad_ref, out_ref):
+def outer_kernel(modes_ref, grads_ref, pred_in, out_far, pred_out, out, sent):
+    pred_out[...] = pred_in[...]
     modes_t = modes_ref[...].T
-    grads = grad_ref[...]
+    grads = grads_ref[...]
     swapped = pltpu.roll(grads, CHANNELS, 1) * lane_sign(grads.shape)
-    for m in range(OUTER):
-        out_ref[m] = (
-            modes_t[0:64, m : m + 1] * grads[m : m + 1]
-            + modes_t[64:128, m : m + 1] * swapped[m : m + 1]
-        )
-
-
-def outer(modes, grads):
+    copies = []
+    for k in range(64 // OUTER):
+        for m in range(k * OUTER, (k + 1) * OUTER):
+            out[m] = (
+                modes_t[0:64, m : m + 1] * grads[m : m + 1]
+                + modes_t[64:128, m : m + 1] * swapped[m : m + 1]
+            )
+        here = pl.ds(k * OUTER, OUTER)
+        copies.append(pltpu.make_async_copy(out.at[here], out_far.at[here], sent.at[k]))
+        copies[-1].start()
+    for copy in copies:
+        copy.wait()
+
+
+def outer(modes, grads, pred):
+    whole = pl.BlockSpec(memory_space=pltpu.VMEM)
     return pl.pallas_call(
         outer_kernel,
-        grid=(64 // OUTER,),
-        out_shape=jax.ShapeDtypeStruct((64, 64, 128), F32),
-        in_specs=[pl.BlockSpec((OUTER, 128), lambda i: (i, 0))] * 2,
-        out_specs=pl.BlockSpec((OUTER, 64, 128), lambda i: (i, 0, 0)),
+        out_shape=(
+            jax.ShapeDtypeStruct((64, 64, 128), F32),
+            jax.ShapeDtypeStruct(pred.shape, F32),
+        ),
+        in_specs=[whole] * 3,
+        out_specs=(pl.BlockSpec(memory_space=pl.ANY), whole),
+        scratch_shapes=[
+            pltpu.VMEM((64, 64, 128), F32), pltpu.SemaphoreType.DMA((64 // OUTER,))
+        ],
         compiler_params=pltpu.CompilerParams(vmem_limit_bytes=VMEM_LIMIT),
         name="outer",
-    )(modes, grads)
+    )(modes, grads, pred)
 
 
 def body(
@@ -689,7 +730,8 @@
         jnp.asarray(kron_forward_y()), jnp.asarray(kron_forward_x()),
         jnp.asarray(kron_inverse_x()), jnp.asarray(kron_inverse_y()),
     )
-    return pred, outer(modes, grads).reshape(32, 2, 1, 64, 128)
+    gradient, pred = outer(modes, grads, pred)
+    return pred, gradient.reshape(32, 2, 1, 64, 128)
 
 
 def solution(mesh):

time: 114 us -> 110 us (0.965)
  Pallas kernels: 112 us -> 108 us
    pallas_call x1, Pallas kernels: 109 us -> 105 us  [step(): pl.pallas_call(step_kernel, out_shape=tuple((jax.ShapeDtypeStruct(*v) for...]
where the time goes in v5:
time: 110 us
  Pallas kernels  108 us (98%)
  between operations  1.45 us (1%)
    pallas_call x1, Pallas kernels, step(): pl.pallas_call(step_kernel, out_shape=tuple((jax.ShapeDtypeStruct(*v) for...  105 us
    pallas_call x1, Pallas kernels, outer(): pl.pallas_call(outer_kernel, out_shape=(jax.ShapeDtypeStruct((64, 64, 128...  3.55 us

profile of v5, /device:TPU:1, one launch (start us, length us, event | category | flops | bytes accessed | tf_op | source)
XLA Modules:
  0.0 109.9 jit_solution(14284018603533244976)
XLA Ops:
  1.3 104.9 %training_step.1 = (f32[1,2048]{1,0:T(1,128)}, f32[64,128]{1,0:T(8,128)}, f32[64,128]{1,0:T(8,128)}) custom-call(bf16[64,1024]{1,0:T(8,128)(2,1)} %bitcast.14, bf16[3,1024]{1,0:T(4,128)(2,1)} %bitcast.17, bf16[8,128]{1,0:T(8,128)(2,1)} %bitcast.19, s32[1,1024]{1,0:T(1,128)} %bitcast.18, s32[1]{0:T(128)S(6)} %copy.25.refs_4_, s32[8,4,2048]{2,1,0:T(4,128)} %refs_5_.1, ...), custom_call_target="tpu_custom_call" | custom-call | tf_op jit(solution)/shard_map/training_step/pallas_call | solution.py:669
  106.2 3.6 %outer.1 = (f32[64,64,128]{2,1,0:T(8,128)}, f32[1,2048]{1,0:T(1,128)}) custom-call(f32[64,128]{1,0:T(8,128)} %get-tuple-element.7.modes_ref, f32[64,128]{1,0:T(8,128)} %get-tuple-element.8.grads_ref, f32[1,2048]{1,0:T(1,128)} %get-tuple-element.9.pred_in), custom_call_target="tpu_custom_call" | custom-call | tf_op jit(solution)/shard_map/outer/pallas_call | solution.py:703

commit v6 on v5

--- a/solution.py
+++ b/solution.py
@@ -26,7 +26,7 @@
 ENC_COLUMNS = 2
 PREP = 512
 OUTER = 16
-POST = 2048
+POST = 4096
 
 
 def frequencies():
@@ -298,10 +298,13 @@
         r.living[h : h + 1, half : half + 128] = extra[7:8]
 
 
-def fetches(r):
+def fetches(r, names):
+    order = list(FETCHED)
     return [
-        pltpu.make_async_copy(getattr(r, name + "_far"), getattr(r, name), r.fetched.at[k])
-        for k, name in enumerate(FETCHED)
+        pltpu.make_async_copy(
+            getattr(r, name + "_far"), getattr(r, name), r.fetched.at[order.index(name)]
+        )
+        for name in names
     ]
 
 
@@ -373,9 +376,10 @@
         rows = [step * ENC_COLUMNS + k for k in range(ENC_COLUMNS)]
         low = jnp.concatenate([r.low[pl.ds(row, 1), :] for row in rows], 1)
         high = jnp.concatenate([r.high[pl.ds(row, 1), :] for row in rows], 1)
+        cells = lax.broadcasted_iota(jnp.int32, (256, n), 0).astype(F32).astype(BF)
         hot = jnp.where(
-            lax.broadcasted_iota(jnp.int32, (256, n), 0) == low, 1.0, 0.0
-        ).astype(BF)
+            cells == low.astype(F32).astype(BF), jnp.asarray(1.0, BF), jnp.asarray(0.0, BF)
+        )
         found = mm(r.table[...], hot)
         high8 = jnp.broadcast_to(high, (8, n))
         near = jnp.zeros((8, 8, n), F32)
@@ -398,7 +402,7 @@
             r.prod[pl.ds(row, 64), :] = shares[:, k * 2048 : (k + 1) * 2048]
         return carry
 
-    lax.fori_loop(0, COLUMNS // ENC_COLUMNS, columns, 0, unroll=2)
+    lax.fori_loop(0, COLUMNS // ENC_COLUMNS, columns, 0, unroll=4)
     shares = 1.0 / r.counts[...]
     group = 8
     for g in range(COLUMNS // group):
@@ -472,11 +476,12 @@
 
     def block(step, carry):
         here = pl.ds(pl.multiple_of(step * n, n), n)
-        cells = r.lists[:, here]
-        low, column = cells & 255, cells >> 8
+        ids = r.lists[:, here]
+        low, column = ids & 255, ids >> 8
+        cells = lax.broadcasted_iota(jnp.int32, (256, n), 0).astype(F32).astype(BF)
         hot = jnp.where(
-            lax.broadcasted_iota(jnp.int32, (256, n), 0) == low, 1.0, 0.0
-        ).astype(BF)
+            cells == low.astype(F32).astype(BF), jnp.asarray(1.0, BF), jnp.asarray(0.0, BF)
+        )
         tw = mm(r.waves[...], hot)
         match = lax.broadcasted_iota(jnp.int32, (COLUMNS, n), 0) == column
         for q in range(32):
@@ -496,11 +501,12 @@
             r.extra[step >> 1].astype(BF),
             r.pairs[pl.ds(pl.multiple_of(half_block * n, n), n), :],
         )
-        cells = r.lists[:, pl.ds(off, n)]
-        low, column = cells & 255, cells >> 8
+        ids = r.lists[:, pl.ds(off, n)]
+        low, column = ids & 255, ids >> 8
+        cells = lax.broadcasted_iota(jnp.int32, (256, n), 0).astype(F32).astype(BF)
         hot = jnp.where(
-            lax.broadcasted_iota(jnp.int32, (256, n), 0) == low, 1.0, 0.0
-        ).astype(BF)
+            cells == low.astype(F32).astype(BF), jnp.asarray(1.0, BF), jnp.asarray(0.0, BF)
+        )
         found = mm(r.lat[...], hot)
         column8 = jnp.broadcast_to(column, (8, n))
         near = jnp.zeros((8, 8, n), F32)
@@ -594,14 +600,17 @@
 
 WIDE, NARROW, POINT_BLOCK = (GROUP, COLUMNS, 128), (GROUP, 16, 128), (GROUP, 80, 128)
 INPUTS = (
-    "features", "positions", "targets", "route", "live", "nbr", "cnt", "lists",
+    "features", "positions", "targets", "route", "live", "nbr_far", "cnt_far", "lists_far",
     "ein", "ebias", "ewo", "din", "dbias", "dwo", "skip", "readout",
     "waves", "weight_far", "ky_far", "kx_far", "kxi_far", "kyi_far",
 )
 FETCHED = {
-    "weight": (64, 64, 128), "ky": (512, 512), "kx": (128, 256), "kxi": (512, 64),
-    "kyi": (1024, 256),
+    "nbr": ((8, 4, 2048), jnp.int32), "cnt": ((8, 4, 256), jnp.int32),
+    "lists": ((1, 4 * SLOT_TOTAL), jnp.int32), "weight": ((64, 64, 128), BF),
+    "ky": ((512, 512), BF), "kx": ((128, 256), BF), "kxi": ((512, 64), BF),
+    "kyi": ((1024, 256), BF),
 }
+EARLY = ("nbr", "cnt", "lists")
 OUTPUTS = {
     "pred": ((1, SLOT_TOTAL), F32), "modes": ((64, 128), F32), "grads": ((64, 128), F32),
 }
@@ -623,7 +632,7 @@
     "basis": ((1024, 4 * SLOT_TOTAL), BF), "back_t": ((64, 1024), BF),
     "dots": ((8, 1024), F32), "total": ((512, 64), F32), "shares": ((64, 4 * SLOT_TOTAL), BF),
     "grad_z": (WIDE, BF), "recv_e": (WIDE, BF), "send_f": (NARROW, BF), "recv_f": (NARROW, BF),
-    **{name: (shape, BF) for name, shape in FETCHED.items()},
+    **FETCHED,
 }
 EXCHANGES = 8
 
@@ -636,16 +645,18 @@
     r = types.SimpleNamespace(**dict(zip(names, refs)))
 
     def before_points():
+        for fetch in fetches(r, EARLY):
+            fetch.wait()
         group_sums(r)
         first_layers(r)
         place_lists(r)
 
-    for fetch in fetches(r):
+    for fetch in fetches(r, FETCHED):
         fetch.start()
     send_points(r, lambda k: before_points if k == 0 else lambda: depth_basis(r))
     slot_tables(r)
     encode(r)
-    for fetch in fetches(r):
+    for fetch in fetches(r, [name for name in FETCHED if name not in EARLY]):
         fetch.wait()
     blocks = 4 * SLOT_TOTAL // PREP // 4
     fourier(r, lambda k: lambda: prepare(r, k * blocks, (k + 1) * blocks))

time: 110 us -> 107 us (0.973)
  Pallas kernels: 108 us -> 105 us
    pallas_call x1, Pallas kernels: 105 us -> 102 us  [step(): pl.pallas_call(step_kernel, out_shape=tuple((jax.ShapeDtypeStruct(*v) for...]
where the time goes in v6:
time: 107 us
  Pallas kernels  105 us (98%)
  between operations  1.45 us (1%)
    pallas_call x1, Pallas kernels, step(): pl.pallas_call(step_kernel, out_shape=tuple((jax.ShapeDtypeStruct(*v) for...  102 us
    pallas_call x1, Pallas kernels, outer(): pl.pallas_call(outer_kernel, out_shape=(jax.ShapeDtypeStruct((64, 64, 128...  3.55 us

profile of v6, /device:TPU:1, one launch (start us, length us, event | category | flops | bytes accessed | tf_op | source)
XLA Modules:
  0.0 106.6 jit_solution(6766467414771801635)
XLA Ops:
  1.3 101.6 %training_step.1 = (f32[1,2048]{1,0:T(1,128)}, f32[64,128]{1,0:T(8,128)}, f32[64,128]{1,0:T(8,128)}) custom-call(bf16[64,1024]{1,0:T(8,128)(2,1)} %bitcast.14, bf16[3,1024]{1,0:T(4,128)(2,1)} %bitcast.17, bf16[8,128]{1,0:T(8,128)(2,1)} %bitcast.19, s32[1,1024]{1,0:T(1,128)} %bitcast.18, s32[1]{0:T(128)S(6)} %copy.25.refs_4_, s32[8,4,2048]{2,1,0:T(4,128)} %refs_5_.1, ...), custom_call_target="tpu_custom_call" | custom-call | tf_op jit(solution)/shard_map/training_step/pallas_call | solution.py:680
  102.9 3.6 %outer.1 = (f32[64,64,128]{2,1,0:T(8,128)}, f32[1,2048]{1,0:T(1,128)}) custom-call(f32[64,128]{1,0:T(8,128)} %get-tuple-element.7.modes_ref, f32[64,128]{1,0:T(8,128)} %get-tuple-element.8.grads_ref, f32[1,2048]{1,0:T(1,128)} %get-tuple-element.9.pred_in), custom_call_target="tpu_custom_call" | custom-call | tf_op jit(solution)/shard_map/outer/pallas_call | solution.py:714
